TPU v7x, 256 devices: a whole 4x4x8 slice. The times are simulated.
256 devices in a mesh: row: 32 (over z, x), col: 8 (over y, core).
Axes of the slice: x: 4, y: 4, z: 8, core: 2. Of those that a mesh axis runs over, the one named last changes fastest.
Arguments:
- density: float32 [3, 4194304], P(None, ('row', 'col')), may hold values from -6 to 6
- interp_weight: float32 [27, 4194304], P(None, ('row', 'col')), may hold values from -1.2 to 1.2
- proj_weight: float32 [27, 4194304], P(None, ('row', 'col')), may hold values from -1.2 to 1.2
- stencil_corner: int32 [3, 32768], P(None, ('row', 'col')), may hold values from 0 to 253, as said below
- near_tiles: bfloat16 [3072, 3, 3, 128, 128], P(('row', 'col')), may hold values from -0.1875 to 0.1875
- pair_target: int32 [3072], P(('row', 'col')), may hold values from 0 to 127
- pair_landing: int32 [3072], P(('row', 'col')), may hold values from 0 to 127
- pair_count: int32 [256], P(('row', 'col')), may hold values from 4 to 12, as said below
Outputs:
- traction_adjoint: float32 [3, 4194304], P(None, ('row', 'col'))
Inputs may be any that keep to these rules, and one draw needn't show every extreme that they name: `stencil_corner`: the stencil of a cluster held by the device with row index r and col index c lies in cells r * 8 to r * 8 + 7 of the first dimension and c * 32 to c * 32 + 31 of the second; every stencil lies inside the grid. `pair_count`: slots at or beyond a device's count are padding; the most is reached on some device in every draw.
All inputs are finite; a program needn't handle non-finite values.
Results may differ from a plain program's by a relative error of at most 0.0003.
Values sent between devices are 32-bit elements; how exact they have to be, the bound alone decides.
A program may use at most 128 MiB of HBM per device.

v0:
```python
import math

import jax
import jax.numpy as jnp
import ml_dtypes
import numpy as np
from jax import lax
from jax.experimental import pallas as pl
from jax.experimental.pallas import tpu as pltpu
from jax.sharding import PartitionSpec as P

G = 256
STENCIL = 27
ROWS = 32
COLS = 8
CLUSTERS = 128
PANELS = 128
SLOTS = 12
BF16 = jnp.bfloat16
F32 = jnp.float32
MESH = pl.DeviceIdType.MESH
FACTOR = 1.0 / math.sqrt(ROWS * COLS * CLUSTERS * PANELS)


def halves(table):
    table = np.asarray(table, np.float64)
    high = table.astype(np.float32).astype(ml_dtypes.bfloat16)
    low = (table - high.astype(np.float64)).astype(np.float32).astype(ml_dtypes.bfloat16)
    return np.stack([high, low])


def rotation(theta):
    cosine, sine = np.cos(theta), np.sin(theta)
    return np.array([[cosine, sine], [-sine, cosine]])


def make_tables():
    two_pi = 2 * np.pi
    bins, cells = np.arange(128), np.arange(G)
    theta = two_pi * (bins[:, None] * cells[None, :] % G) / G
    line = np.stack([np.cos(theta), -np.sin(theta)]).reshape(2, COLS, 16, G)
    line = line.transpose(1, 0, 2, 3).reshape(G, G)
    eight = np.arange(8)
    wide = np.arange(32)
    turn8 = rotation(two_pi * (eight[:, None] * eight[None, :] % 8) / 8)
    turn32 = rotation(two_pi * (wide[:, None] * wide[None, :] % 32) / 32)
    second = np.einsum("oipc,hg,lm->phol" "cigm", turn8, np.eye(4), np.eye(4)).reshape(G, G)
    first = np.einsum("oipr,lm->polrim", turn32, np.eye(4)).reshape(G, G)
    lane32 = [np.kron(np.eye(8), f(two_pi * (wide[:, None] * wide[None, :] % 32) / 32)) for f in (np.cos, np.sin)]
    lane8 = [np.kron(f(two_pi * (eight[:, None] * eight[None, :] % 8) / 8), np.eye(32)) for f in (np.cos, np.sin)]
    row = np.arange(G)
    lane = np.arange(G)
    part_sign = np.where(row // 4 % 2 == 0, 1.0, -1.0)[:, None]
    twist_y = two_pi * ((row // 32)[:, None] * (lane % 32)[None, :]) / G
    twist_x = two_pi * ((row // 8)[:, None] * (lane // 32)[None, :]) / G
    twiddle = np.stack(
        [np.cos(twist_y), part_sign * np.sin(twist_y), np.cos(twist_x), part_sign * np.sin(twist_x)]
    ).astype(np.float32)
    rows_table = np.stack([halves(t) for t in (second, first, first.T, second.T)])
    lanes_table = np.stack([halves(np.concatenate(t, axis=1)) for t in (lane32, lane8)])
    return halves(line), rows_table, lanes_table, twiddle


def split(values):
    high = values.astype(BF16)
    return high, (values - high.astype(F32)).astype(BF16)


def mm(a, b):
    return jnp.dot(a, b, preferred_element_type=F32)


def mm_nt(a, b):
    return lax.dot_general(a, b, (((1,), (1,)), ((), ())), preferred_element_type=F32)


def swap(values):
    grouped = values.reshape(32, 8, values.shape[1])
    return pltpu.roll(grouped, 4, 1).reshape(values.shape)


def on_rows(table_high, table_low, values):
    high, low = split(values)
    return mm(table_high, high) + (mm(table_low, high) + mm(table_high, low))


def on_lanes(values, table_high, table_low, sign):
    high, low = split(values)
    both = mm(high, table_high) + (mm(low, table_high) + mm(high, table_low))
    return both[:, :G] + sign * swap(both[:, G:])


def signs(direction):
    row = lax.broadcasted_iota(jnp.int32, (G, G), 0)
    return jnp.where((row & 4) == 0, direction, -direction).astype(F32)


def forward(values, rows_high, rows_low, lanes_high, lanes_low, cosines, sines):
    values = on_rows(rows_high, rows_low, values)
    values = values * cosines + swap(values) * sines
    return on_lanes(values, lanes_high, lanes_low, signs(1.0))


def backward(values, rows_high, rows_low, lanes_high, lanes_low, cosines, sines):
    values = on_lanes(values, lanes_high, lanes_low, signs(-1.0))
    values = values * cosines - swap(values) * sines
    return on_rows(rows_high, rows_low, values)


def wave(index):
    return jnp.where(index < G // 2, index, index - G).astype(F32)


def wavevector(row_index, col_index):
    row = lax.broadcasted_iota(jnp.int32, (G, G), 0)
    lane = lax.broadcasted_iota(jnp.int32, (G, G), 1)
    m1 = (row >> 3) + (lane & -32)
    m2 = row_index // 4 + 8 * (lane & 31)
    m3 = 16 * col_index + 4 * (row_index % 4) + (row & 3)
    return m1, m2, m3


def screen(row_index, col_index):
    m1, m2, m3 = wavevector(row_index, col_index)
    w1, w2, w3 = wave(m1), wave(m2), m3.astype(F32)
    squared = w1 * w1 + w2 * w2 + w3 * w3
    kept = jnp.where((m1 == G // 2) | (m2 == G // 2), 0.0, FACTOR).astype(F32)
    fold = jnp.where(m3 == 0, 1.0, 2.0).astype(F32)
    return w1, w2, w3, 1.0 / jnp.maximum(squared, 1.0), kept * fold / (squared + 0.5)


def spread_kernel(density, weight, corner, line, target, count, grid, phases, hot, picked, upper, lower):
    row_index, col_index = lax.axis_index("row"), lax.axis_index("col")
    lane = lax.broadcasted_iota(jnp.int32, (STENCIL, CLUSTERS), 1)
    group = 8

    def gather_sums(i, sums):
        start = pl.multiple_of(i * group * PANELS, group * PANELS)
        block = weight[:, pl.ds(start, group * PANELS)]
        charge = density[:, pl.ds(start, group * PANELS)]
        sums = list(sums)
        for c in range(3):
            product = block * charge[c : c + 1]
            for k in range(group):
                total = jnp.sum(product[:, k * PANELS : (k + 1) * PANELS], axis=1, keepdims=True)
                sums[c] = jnp.where(lane == i * group + k, total, sums[c])
        return tuple(sums)

    picked[...] = jnp.zeros_like(picked)
    live = count[0]
    for q in range(SLOTS):
        start = pl.multiple_of(target[q] * PANELS, PANELS)
        charge = density[:, pl.ds(start, PANELS)].astype(BF16).astype(F32)
        picked[q, 0:3] = jnp.where(q < live, charge, jnp.zeros_like(charge))

    zero = jnp.zeros((STENCIL, CLUSTERS), F32)
    sums = lax.fori_loop(0, CLUSTERS // group, gather_sums, (zero,) * 3)

    corners = corner[...]
    local = (corners[0:1] - row_index * 8) * 32 + (corners[1:2] - col_index * 32)
    cell = lax.broadcasted_iota(jnp.int32, (G, CLUSTERS), 0)
    for dz in range(3):
        at = jnp.where(cell == corners[2:3] + dz, 1.0, 0.0).astype(BF16)
        phases[dz] = mm(line[0], at) + mm(line[1], at)
    for d in range(9):
        here = jnp.where(cell == local + (d // 3 * 32 + d % 3), 1.0, 0.0).astype(BF16)
        hot[:, d * CLUSTERS : (d + 1) * CLUSTERS] = here
    for c in range(3):
        for d in range(9):
            value = phases[0] * sums[c][3 * d : 3 * d + 1]
            value += phases[1] * sums[c][3 * d + 1 : 3 * d + 2]
            value += phases[2] * sums[c][3 * d + 2 : 3 * d + 3]
            high, low = split(value)
            upper[:, d * CLUSTERS : (d + 1) * CLUSTERS] = high
            lower[:, d * CLUSTERS : (d + 1) * CLUSTERS] = low
        total = mm_nt(upper[...], hot[...]) + mm_nt(lower[...], hot[...])
        grid[c] = total.reshape(COLS, 32, G)


def exchange_kernel(
    sent1, rows_table, lanes_table, twiddle, picked, tiles,
    got4, near_here, near_got,
    got1, sent2, got2, modes, sent3, got3, sent4, near_sent, blocks,
    send_sem, recv_sem, near_sem, tile_sem,
):
    row_index, col_index = lax.axis_index("row"), lax.axis_index("col")
    tile_copy = pltpu.make_async_copy(tiles, blocks, tile_sem)
    tile_copy.start()

    barrier = pltpu.get_barrier_semaphore()

    def row_peer(j):
        return lax.rem(row_index + j, ROWS)

    def col_peer(j):
        return lax.rem(col_index + j, COLS)

    def greet_row(j, carry):
        pl.semaphore_signal(barrier, inc=1, device_id=(row_peer(j), col_index), device_id_type=MESH)
        return carry

    def greet_col(j, carry):
        pl.semaphore_signal(barrier, inc=1, device_id=(row_index, col_peer(j)), device_id_type=MESH)
        return carry

    lax.fori_loop(1, COLS, greet_col, 0)
    lax.fori_loop(1, ROWS, greet_row, 0)
    pl.semaphore_wait(barrier, COLS + ROWS - 2)

    def to_cols(stage, source, target_ref, c):
        def one(j, carry):
            peer = col_peer(j)
            pltpu.make_async_remote_copy(
                source.at[c, peer],
                target_ref.at[c, col_index],
                send_sem.at[stage, c],
                recv_sem.at[stage, c],
                device_id=(row_index, peer),
                device_id_type=MESH,
            ).start()
            return carry

        lax.fori_loop(1, COLS, one, 0)
        target_ref[c, col_index] = source[c, col_index]

    def to_rows(stage, source, target_ref, c):
        def one(j, carry):
            peer = row_peer(j)
            pltpu.make_async_remote_copy(
                source.at[c, peer],
                target_ref.at[c, row_index],
                send_sem.at[stage, c],
                recv_sem.at[stage, c],
                device_id=(peer, col_index),
                device_id_type=MESH,
            ).start()
            return carry

        lax.fori_loop(1, ROWS, one, 0)
        target_ref[c, row_index] = source[c, row_index]

    def whole(stage, source, target_ref, c):
        peers = source.shape[1] - 1
        return pltpu.make_async_remote_copy(
            source.at[c, pl.ds(0, peers)],
            target_ref.at[c, pl.ds(0, peers)],
            send_sem.at[stage, c],
            recv_sem.at[stage, c],
            device_id=(row_peer(1), col_index),
            device_id_type=MESH,
        )

    def rows_of(k):
        return rows_table[k, 0], rows_table[k, 1]

    def lanes_of(k):
        return lanes_table[k, 0], lanes_table[k, 1]

    def start1(c, carry):
        to_cols(0, sent1, got1, c)
        return carry

    lax.fori_loop(0, 3, start1, 0)

    def second_dimension(c, carry):
        whole(0, sent1, got1, c).wait_recv()
        values = forward(got1[c].reshape(G, G), *rows_of(0), *lanes_of(0), twiddle[0], twiddle[1])
        sent2[c] = values.reshape(ROWS, 8, G)
        to_rows(1, sent2, got2, c)
        return carry

    lax.fori_loop(0, 3, second_dimension, 0)

    tile_copy.wait()

    near_sent[...] = jnp.zeros_like(near_sent)

    def slot(q, carry):
        charge = picked[q].astype(BF16)
        for b in range(3):
            total = mm(charge[0:1], blocks[q, 0, b])
            total += mm(charge[1:2], blocks[q, 1, b])
            total += mm(charge[2:3], blocks[q, 2, b])
            near_sent[q, b : b + 1] = total
        return carry

    lax.fori_loop(0, SLOTS, slot, 0)
    near_here[...] = near_sent[0:4]
    near_copies = []
    for side, peer in ((0, row_peer(ROWS - 1)), (1, row_peer(1))):
        for k in range(4):
            near_copies.append(
                pltpu.make_async_remote_copy(
                    near_sent.at[4 + 2 * k + side],
                    near_got.at[2 * k + side],
                    near_sem.at[0, 2 * k + side],
                    near_sem.at[1, 2 * k + side],
                    device_id=(peer, col_index),
                    device_id_type=MESH,
                )
            )
    for copy in near_copies:
        copy.start()

    w1, w2, w3, inverse, weighting = screen(row_index, col_index)

    def first_dimension(c, carry):
        whole(1, sent2, got2, c).wait_recv()
        modes[c] = forward(got2[c].reshape(G, G), *rows_of(1), *lanes_of(1), twiddle[2], twiddle[3])
        return carry

    lax.fori_loop(0, 3, first_dimension, 0)

    inner = (w1 * modes[0] + w2 * modes[1] + w3 * modes[2]) * inverse
    for c, w in enumerate((w1, w2, w3)):
        modes[c] = (modes[c] - w * inner) * weighting

    def first_back(c, carry):
        values = backward(modes[c], *rows_of(2), *lanes_of(1), twiddle[2], twiddle[3])
        sent3[c] = values.reshape(ROWS, 8, G)
        to_rows(2, sent3, got3, c)
        return carry

    lax.fori_loop(0, 3, first_back, 0)

    def second_back(c, carry):
        whole(2, sent3, got3, c).wait_recv()
        values = backward(got3[c].reshape(G, G), *rows_of(3), *lanes_of(0), twiddle[0], twiddle[1])
        sent4[c] = values.reshape(COLS, 32, G)
        to_cols(3, sent4, got4, c)
        return carry

    lax.fori_loop(0, 3, second_back, 0)

    for copy in near_copies:
        copy.wait()

    def finish(c, carry):
        whole(3, sent4, got4, c).wait()
        whole(0, sent1, got1, c).wait_send()
        whole(1, sent2, got2, c).wait_send()
        whole(2, sent3, got3, c).wait_send()
        return carry

    lax.fori_loop(0, 3, finish, 0)


def project_kernel(got4, phases, hot, weight, near_here, near_got, landing, out, mixed, values):
    values[...] = jnp.zeros_like(values)
    for c in range(3):
        high, low = split(got4[c].reshape(G, G))
        mixed[...] = mm(high, hot[...]) + mm(low, hot[...])
        for d in range(9):
            part = mixed[:, d * CLUSTERS : (d + 1) * CLUSTERS]
            for dz in range(3):
                values[c, 3 * d + dz : 3 * d + dz + 1] = jnp.sum(part * phases[dz], axis=0, keepdims=True)
    group = 8

    def clusters(i, carry):
        start = pl.multiple_of(i * group * PANELS, group * PANELS)
        block = weight[:, pl.ds(start, group * PANELS)]
        shift = lax.rem(CLUSTERS - i * group, CLUSTERS)
        for c in range(3):
            turned = pltpu.roll(values[c], shift, 1)
            for k in range(group):
                product = block[:, k * PANELS : (k + 1) * PANELS] * turned[:STENCIL, k : k + 1]
                place = pl.multiple_of(start + k * PANELS, PANELS)
                out[c : c + 1, pl.ds(place, PANELS)] = jnp.sum(product, axis=0, keepdims=True)
        return carry

    lax.fori_loop(0, CLUSTERS // group, clusters, 0)
    for q in range(SLOTS):
        place = pl.multiple_of(landing[q] * PANELS, PANELS)
        arrived = near_here[q] if q < 4 else near_got[q - 4]
        out[:, pl.ds(place, PANELS)] += arrived[:3]


VMEM = pl.BlockSpec(memory_space=pltpu.VMEM)
SMEM = pl.BlockSpec(memory_space=pltpu.SMEM)
ANY = pl.BlockSpec(memory_space=pl.ANY)
LIMIT = 48 * 1024 * 1024


def shape(dims, dtype=F32):
    return jax.ShapeDtypeStruct(dims, dtype)


def per_device(
    density, interp_weight, proj_weight, stencil_corner, near_tiles, pair_target, pair_landing, pair_count
):
    line, rows_table, lanes_table, twiddle = (jnp.asarray(t) for t in make_tables())
    by_cols, by_rows = (3, COLS, 32, G), (3, ROWS, 8, G)
    grid, phases, hot, picked = pl.pallas_call(
        spread_kernel,
        out_shape=(shape(by_cols), shape((3, G, CLUSTERS)), shape((G, 9 * CLUSTERS), BF16), shape((SLOTS, 8, PANELS))),
        in_specs=[VMEM] * 4 + [SMEM] * 2,
        out_specs=(VMEM,) * 4,
        scratch_shapes=[pltpu.VMEM((G, 9 * CLUSTERS), BF16)] * 2,
        compiler_params=pltpu.CompilerParams(vmem_limit_bytes=LIMIT),
    )(density, interp_weight, stencil_corner, line, pair_target, pair_count)
    got4, near_here, near_got = pl.pallas_call(
        exchange_kernel,
        out_shape=(shape(by_cols), shape((4, 8, PANELS)), shape((8, 8, PANELS))),
        in_specs=[VMEM] * 5 + [ANY],
        out_specs=(VMEM, VMEM, VMEM),
        scratch_shapes=[
            pltpu.VMEM(by_cols, F32),
            pltpu.VMEM(by_rows, F32),
            pltpu.VMEM(by_rows, F32),
            pltpu.VMEM((3, G, G), F32),
            pltpu.VMEM(by_rows, F32),
            pltpu.VMEM(by_rows, F32),
            pltpu.VMEM(by_cols, F32),
            pltpu.VMEM((SLOTS, 8, PANELS), F32),
            pltpu.VMEM((SLOTS, 3, 3, PANELS, PANELS), BF16),
            pltpu.SemaphoreType.DMA((4, 3)),
            pltpu.SemaphoreType.DMA((4, 3)),
            pltpu.SemaphoreType.DMA((2, 8)),
            pltpu.SemaphoreType.DMA,
        ],
        compiler_params=pltpu.CompilerParams(
            vmem_limit_bytes=LIMIT, collective_id=0, has_side_effects=True
        ),
    )(grid, rows_table, lanes_table, twiddle, picked, near_tiles)
    return pl.pallas_call(
        project_kernel,
        out_shape=shape((3, CLUSTERS * PANELS)),
        in_specs=[VMEM] * 6 + [SMEM],
        out_specs=VMEM,
        scratch_shapes=[pltpu.VMEM((G, 9 * CLUSTERS), F32), pltpu.VMEM((3, 32, CLUSTERS), F32)],
        compiler_params=pltpu.CompilerParams(vmem_limit_bytes=LIMIT),
    )(got4, phases, hot, proj_weight, near_here, near_got, pair_landing)


def solution(mesh):
    flat = P(None, ("row", "col"))
    slots = P(("row", "col"))
    in_specs = (flat, flat, flat, flat, P(("row", "col"), None, None, None, None), slots, slots, slots)
    return jax.shard_map(
        per_device, mesh=mesh, in_specs=in_specs, out_specs=flat, check_vma=False
    )
```

profile of v0, /device:TPU:1, one launch (start us, length us, event | category | flops | bytes accessed | tf_op | source)
XLA Modules:
  0.0 89.2 jit_solution(16788795039176835695)
XLA Ops:
  0.7 0.0 copy-start
  0.7 1.6 %copy-done = f32[27,16384]{1,0:T(8,128)S(1)} copy-done((f32[27,16384]{1,0:T(8,128)S(1)}, f32[27,16384]{1,0:T(8,128)}, u32[]{:S(2)}) %copy-start) | copy-done | bytes 1769496
  2.2 0.0 copy-start.5
  2.2 0.9 %copy-done.5 = f32[3,16384]{1,0:T(4,128)S(1)} copy-done((f32[3,16384]{1,0:T(4,128)S(1)}, f32[3,16384]{1,0:T(4,128)}, u32[]{:S(2)}) %copy-start.5) | copy-done | bytes 196632
  3.2 0.0 copy-start.6
  3.2 0.9 %copy-done.6 = bf16[2,256,256]{2,1,0:T(8,128)(2,1)S(1)} copy-done((bf16[2,256,256]{2,1,0:T(8,128)(2,1)S(1)}, bf16[2,256,256]{2,1,0:T(8,128)(2,1)}, u32[]{:S(2)}) %copy-start.6) | copy-done | bytes 262168
  4.1 0.0 copy-start.7
  4.1 0.7 copy-done.7
  4.8 0.0 copy-start.9
  4.8 0.7 copy-done.9
  5.5 0.0 copy-start.2
  5.5 0.0 copy-start.3
  5.5 6.2 %shard_map.118 = (f32[3,8,32,256]{3,2,1,0:T(8,128)S(1)}, f32[3,256,128]{2,1,0:T(8,128)S(1)}, bf16[256,1152]{1,0:T(8,128)(2,1)S(1)}, f32[12,8,128]{2,1,0:T(8,128)S(1)}) custom-call(f32[3,16384]{1,0:T(4,128)S(1)} %copy-done.5, f32[27,16384]{1,0:T(8,128)S(1)} %copy-done, s32[3,128]{1,0:T(4,128)S(1)} %copy-done.7, bf16[2,256,256]{2,1,0:T(8,128)(2,1)S(1)} %copy-done.6, ...), custom_call_target="tpu_custom_call" | custom-call | tf_op jit(solution)/shard_map/pallas_call | solution.py:393
  11.7 0.0 copy-done.2
  11.7 0.0 copy-done.3
  11.7 0.0 copy-start.4
  11.7 1.2 %copy-done.4 = bf16[4,2,256,256]{3,2,1,0:T(8,128)(2,1)S(1)} copy-done((bf16[4,2,256,256]{3,2,1,0:T(8,128)(2,1)S(1)}, bf16[4,2,256,256]{3,2,1,0:T(8,128)(2,1)}, u32[]{:S(2)}) %copy-start.4) | copy-done | bytes 1048600
  12.9 0.0 copy-start.1
  12.9 0.0 copy-start.8
  12.9 67.7 %shard_map.119 = (f32[3,8,32,256]{3,2,1,0:T(8,128)S(1)}, f32[4,8,128]{2,1,0:T(8,128)S(1)}, f32[8,8,128]{2,1,0:T(8,128)S(1)}) custom-call(f32[3,8,32,256]{3,2,1,0:T(8,128)S(1)} %get-tuple-element.12.sent1, bf16[4,2,256,256]{3,2,1,0:T(8,128)(2,1)S(1)} %copy-done.4, bf16[2,2,256,512]{3,2,1,0:T(8,128)(2,1)S(1)} %copy-done.3, f32[4,256,256]{2,1,0:T(8,128)S(1)} %copy-done.2, ...), custom_call_target="tpu_custom_call" | custom-call | tf_op jit(solution)/shard_map/pallas_call | solution.py:401
  80.7 0.0 copy-done.1
  80.7 0.0 copy-done.8
  80.7 8.5 %shard_map.120 = f32[3,16384]{1,0:T(4,128)} custom-call(f32[3,8,32,256]{3,2,1,0:T(8,128)S(1)} %get-tuple-element.14.got4, f32[3,256,128]{2,1,0:T(8,128)S(1)} %get-tuple-element.15.phases, bf16[256,1152]{1,0:T(8,128)(2,1)S(1)} %get-tuple-element.16.hot, f32[27,16384]{1,0:T(8,128)S(1)} %copy-done.1, f32[4,8,128]{2,1,0:T(8,128)S(1)} %get-tuple-element.17.near_here, ...), custom_call_target="tpu_custom_call" | custom-call | tf_op jit(solution)/shard_map/pallas_call | solution.py:425
Async XLA Ops:
  0.7 1.6 %copy-start = (f32[27,16384]{1,0:T(8,128)S(1)}, f32[27,16384]{1,0:T(8,128)}, u32[]{:S(2)}) copy-start(f32[27,16384]{1,0:T(8,128)} %weight.2) | copy-start | bytes 5308420
  2.2 0.9 %copy-start.5 = (f32[3,16384]{1,0:T(4,128)S(1)}, f32[3,16384]{1,0:T(4,128)}, u32[]{:S(2)}) copy-start(f32[3,16384]{1,0:T(4,128)} %density.1) | copy-start | bytes 589828
  3.2 0.9 %copy-start.6 = (bf16[2,256,256]{2,1,0:T(8,128)(2,1)S(1)}, bf16[2,256,256]{2,1,0:T(8,128)(2,1)}, u32[]{:S(2)}) copy-start(bf16[2,256,256]{2,1,0:T(8,128)(2,1)} %constant.8.clone.line) | copy-start | bytes 786436
  4.1 0.7 copy-start.7
  4.8 0.7 copy-start.9
  5.5 6.2 %copy-start.2 = (f32[4,256,256]{2,1,0:T(8,128)S(1)}, f32[4,256,256]{2,1,0:T(8,128)}, u32[]{:S(2)}) copy-start(f32[4,256,256]{2,1,0:T(8,128)} %constant.11.clone.twiddle) | copy-start | bytes 3145732
  5.5 6.2 %copy-start.3 = (bf16[2,2,256,512]{3,2,1,0:T(8,128)(2,1)S(1)}, bf16[2,2,256,512]{3,2,1,0:T(8,128)(2,1)}, u32[]{:S(2)}) copy-start(bf16[2,2,256,512]{3,2,1,0:T(8,128)(2,1)} %constant.10.clone.lanes_table) | copy-start | bytes 3145732
  11.7 1.2 %copy-start.4 = (bf16[4,2,256,256]{3,2,1,0:T(8,128)(2,1)S(1)}, bf16[4,2,256,256]{3,2,1,0:T(8,128)(2,1)}, u32[]{:S(2)}) copy-start(bf16[4,2,256,256]{3,2,1,0:T(8,128)(2,1)} %constant.9.clone.rows_table) | copy-start | bytes 3145732
  12.9 67.7 %copy-start.1 = (f32[27,16384]{1,0:T(8,128)S(1)}, f32[27,16384]{1,0:T(8,128)}, u32[]{:S(2)}) copy-start(f32[27,16384]{1,0:T(8,128)} %weight.3) | copy-start | bytes 5308420
  12.9 67.7 %copy-start.8 = (s32[12]{0:T(128)S(1)}, s32[12]{0:T(128)}, u32[]{:S(2)}) copy-start(s32[12]{0:T(128)} %landing.1) | copy-start | bytes 148
where the time goes:
time: 89.5 us; the launch traced here: 89.2 us
  Pallas kernels  82.4 us (92%)
  local copies, waits for them, and re-layouts  6.05 us (7%)
    pallas_call x1, Pallas kernels, per_device(): pl.pallas_call(exchange_kernel, out_shape=(shape(by_cols), shape((4, 8, P...  67.7 us
    pallas_call x1, Pallas kernels, per_device(): pl.pallas_call(project_kernel, out_shape=shape((3, CLUSTERS * PANELS)), i...  8.51 us
    pallas_call x1, Pallas kernels, per_device(): pl.pallas_call(spread_kernel, out_shape=(shape(by_cols), shape((3, G, CLU...  6.2 us
    unnamed x20, local copies, waits for them, and re-layouts  6.05 us

commit v1 on v0

v1 whole, which is shorter than its diff:
```python
import math

import jax
import jax.numpy as jnp
import ml_dtypes
import numpy as np
from jax import lax
from jax.experimental import pallas as pl
from jax.experimental.pallas import tpu as pltpu
from jax.sharding import PartitionSpec as P

G = 256
STENCIL = 27
ROWS = 32
COLS = 8
DEPTH = 8
WIDTH = 4
PACKED = 88
CLUSTERS = 128
PANELS = 128
SLOTS = 12
BF16 = jnp.bfloat16
F32 = jnp.float32
MESH = pl.DeviceIdType.MESH
FACTOR = 1.0 / math.sqrt(ROWS * COLS * CLUSTERS * PANELS)


def halves(table):
    table = np.asarray(table, np.float64)
    high = table.astype(np.float32).astype(ml_dtypes.bfloat16)
    low = (table - high.astype(np.float64)).astype(np.float32).astype(ml_dtypes.bfloat16)
    return np.stack([high, low])


def rotation(theta):
    cosine, sine = np.cos(theta), np.sin(theta)
    return np.array([[cosine, sine], [-sine, cosine]])


def make_tables():
    two_pi = 2 * np.pi
    bins, cells = np.arange(128), np.arange(G)
    theta = two_pi * (bins[:, None] * cells[None, :] % G) / G
    line = np.stack([np.cos(theta), -np.sin(theta)]).reshape(2, DEPTH, WIDTH, 4, G)
    line = line.transpose(1, 2, 0, 3, 4).reshape(DEPTH, 32, G)
    line = halves(line).transpose(1, 0, 2, 3).reshape(DEPTH, 64, G)
    eight = np.arange(8)
    wide = np.arange(32)
    turn8 = rotation(two_pi * (eight[:, None] * eight[None, :] % 8) / 8)
    turn32 = rotation(two_pi * (wide[:, None] * wide[None, :] % 32) / 32)
    second = np.einsum("oipc,hg,lm->pholcgim", turn8, np.eye(4), np.eye(4)).reshape(G, G)
    by_block = turn32.reshape(2, 2, 32, DEPTH, WIDTH)
    first = np.einsum("oipzx,lm->polxzim", by_block, np.eye(4)).reshape(G, G)
    lane32 = [np.kron(np.eye(8), f(two_pi * (wide[:, None] * wide[None, :] % 32) / 32)) for f in (np.cos, np.sin)]
    lane8 = [np.kron(f(two_pi * (eight[:, None] * eight[None, :] % 8) / 8), np.eye(32)) for f in (np.cos, np.sin)]
    row = np.arange(G)
    lane = np.arange(G)
    part_sign = np.where(row // 4 % 2 == 0, 1.0, -1.0)[:, None]
    twist_y = two_pi * ((row // 32)[:, None] * (lane % 32)[None, :]) / G
    twist_x = two_pi * ((row // 8)[:, None] * (lane // 32)[None, :]) / G
    twiddle = np.stack(
        [np.cos(twist_y), part_sign * np.sin(twist_y), np.cos(twist_x), part_sign * np.sin(twist_x)]
    ).astype(np.float32)
    rows_table = np.stack([halves(t) for t in (second, first, first.T, second.T)])
    lanes_table = np.stack([halves(np.concatenate(t, axis=1)) for t in (lane32, lane8)])
    return line, rows_table, lanes_table, twiddle


def split(values):
    high = values.astype(BF16)
    return high, (values - high.astype(F32)).astype(BF16)


def mm(a, b):
    return jnp.dot(a, b, preferred_element_type=F32)


def mm_nt(a, b):
    return lax.dot_general(a, b, (((1,), (1,)), ((), ())), preferred_element_type=F32)


def swap(values):
    grouped = values.reshape(32, 8, values.shape[1])
    return pltpu.roll(grouped, 4, 1).reshape(values.shape)


def on_rows(table_high, table_low, values):
    high, low = split(values)
    return mm(table_high, high) + (mm(table_low, high) + mm(table_high, low))


def on_lanes(values, table_high, table_low, sign):
    high, low = split(values)
    both = mm(high, table_high) + (mm(low, table_high) + mm(high, table_low))
    return both[:, :G] + sign * swap(both[:, G:])


def signs(direction):
    row = lax.broadcasted_iota(jnp.int32, (G, G), 0)
    return jnp.where((row & 4) == 0, direction, -direction).astype(F32)


def forward(values, rows_high, rows_low, lanes_high, lanes_low, cosines, sines):
    values = on_rows(rows_high, rows_low, values)
    values = values * cosines + swap(values) * sines
    return on_lanes(values, lanes_high, lanes_low, signs(1.0))


def backward(values, rows_high, rows_low, lanes_high, lanes_low, cosines, sines):
    values = on_lanes(values, lanes_high, lanes_low, signs(-1.0))
    values = values * cosines - swap(values) * sines
    return on_rows(rows_high, rows_low, values)


def wave(index):
    return jnp.where(index < G // 2, index, index - G).astype(F32)


def wavevector(row_index, col_index):
    row = lax.broadcasted_iota(jnp.int32, (G, G), 0)
    lane = lax.broadcasted_iota(jnp.int32, (G, G), 1)
    m1 = 4 * col_index + ((row >> 3) & 3) + (lane & -32)
    m2 = (row >> 5) + 8 * (lane & 31)
    m3 = 4 * row_index + (row & 3)
    return m1, m2, m3


def screen(row_index, col_index):
    m1, m2, m3 = wavevector(row_index, col_index)
    w1, w2, w3 = wave(m1), wave(m2), m3.astype(F32)
    squared = w1 * w1 + w2 * w2 + w3 * w3
    kept = jnp.where((m1 == G // 2) | (m2 == G // 2), 0.0, FACTOR).astype(F32)
    fold = jnp.where(m3 == 0, 1.0, 2.0).astype(F32)
    return w1, w2, w3, 1.0 / jnp.maximum(squared, 1.0), kept * fold / (squared + 0.5)


def spread_kernel(density, weight, corner, target, count, packed, picked):
    row_index, col_index = lax.axis_index("row"), lax.axis_index("col")
    lane = lax.broadcasted_iota(jnp.int32, (STENCIL, CLUSTERS), 1)
    group = 8

    def gather_sums(i, sums):
        start = pl.multiple_of(i * group * PANELS, group * PANELS)
        block = weight[:, pl.ds(start, group * PANELS)]
        charge = density[:, pl.ds(start, group * PANELS)]
        sums = list(sums)
        for c in range(3):
            product = block * charge[c : c + 1]
            for k in range(group):
                total = jnp.sum(product[:, k * PANELS : (k + 1) * PANELS], axis=1, keepdims=True)
                sums[c] = jnp.where(lane == i * group + k, total, sums[c])
        return tuple(sums)

    picked[...] = jnp.zeros_like(picked)
    live = count[0]
    for q in range(SLOTS):
        start = pl.multiple_of(target[q] * PANELS, PANELS)
        charge = density[:, pl.ds(start, PANELS)].astype(BF16).astype(F32)
        picked[q, 0:3] = jnp.where(q < live, charge, jnp.zeros_like(charge))

    zero = jnp.zeros((STENCIL, CLUSTERS), F32)
    sums = lax.fori_loop(0, CLUSTERS // group, gather_sums, (zero,) * 3)

    corners = corner[...]
    local = (corners[0:1] - row_index * 8) * 32 + (corners[1:2] - col_index * 32)
    packed[80:PACKED] = jnp.zeros((PACKED - 80, CLUSTERS), F32)
    for c in range(3):
        packed[c * STENCIL : (c + 1) * STENCIL] = sums[c]
    packed[81:82] = local.astype(F32)
    packed[82:83] = corners[2:3].astype(F32)


def exchange_kernel(
    packed, line, rows_table, lanes_table, twiddle, picked, tiles,
    samples, near_here, near_got,
    gathered, hot, phases, upper, sent1, got1, sent2, got2, modes, sent3, got3, sent4, got4, sent5, got5, near_sent, blocks,
    slab_send, slab_recv, plane_sem, send_sem, recv_sem, near_sem, tile_sem,
):
    row_index, col_index = lax.axis_index("row"), lax.axis_index("col")
    z_index, x_index = row_index // WIDTH, lax.rem(row_index, WIDTH)
    tile_copy = pltpu.make_async_copy(tiles, blocks, tile_sem)
    tile_copy.start()

    def z_peer(j):
        return lax.rem(z_index + j, DEPTH)

    def x_peer(j):
        return lax.rem(x_index + j, WIDTH)

    def col_peer(j):
        return lax.rem(col_index + j, COLS)

    def at_z(peer):
        return (peer * WIDTH + x_index, col_index)

    def at_x(peer):
        return (z_index * WIDTH + peer, col_index)

    def at_col(peer):
        return (row_index, peer)

    def at_row(j):
        return (lax.rem(row_index + j, ROWS), col_index)

    barrier = pltpu.get_barrier_semaphore()

    def greet(device):
        pl.semaphore_signal(barrier, inc=1, device_id=device, device_id_type=MESH)

    def greet_z(j, carry):
        greet(at_z(z_peer(j)))
        return carry

    def greet_x(j, carry):
        greet(at_x(x_peer(j)))
        return carry

    def greet_col(j, carry):
        greet(at_col(col_peer(j)))
        return carry

    lax.fori_loop(1, DEPTH, greet_z, 0)
    lax.fori_loop(1, WIDTH, greet_x, 0)
    lax.fori_loop(1, COLS, greet_col, 0)
    greet(at_row(1))
    greet(at_row(ROWS - 1))
    pl.semaphore_wait(barrier, DEPTH + WIDTH + COLS - 3 + 2)

    def near_first(i):
        odd = lax.rem(i, 2)
        return odd * ((i + 1) // 2) + (1 - odd) * (DEPTH - i // 2)

    def slab_copy(j):
        return pltpu.make_async_remote_copy(
            packed,
            gathered.at[z_index],
            slab_send.at[j],
            slab_recv.at[j],
            device_id=at_z(z_peer(j)),
            device_id_type=MESH,
        )

    def send_slab(i, carry):
        slab_copy(near_first(i)).start()
        return carry

    lax.fori_loop(1, DEPTH, send_slab, 0)
    gathered[z_index] = packed[...]

    def plane_copy(source, target, device):
        return pltpu.make_async_remote_copy(
            source, target, plane_sem.at[0], plane_sem.at[1], device_id=device, device_id_type=MESH
        )

    cell = lax.broadcasted_iota(jnp.int32, (G, CLUSTERS), 0).astype(F32)

    def build(zs):
        local, depth = gathered[zs, 81:82], gathered[zs, 82:83]
        for dz in range(3):
            at = jnp.where(cell == depth + float(dz), 1.0, 0.0).astype(BF16)
            both = mm(line[z_index], at)
            phases[zs, dz] = both[:32] + both[32:]
        for d in range(9):
            here = jnp.where(cell == local + float(d // 3 * 32 + d % 3), 1.0, 0.0).astype(BF16)
            hot[zs, :, d * CLUSTERS : (d + 1) * CLUSTERS] = here
        for c in range(3):
            for d in range(9):
                at = c * STENCIL + 3 * d
                value = phases[zs, 0] * gathered[zs, at : at + 1]
                value += phases[zs, 1] * gathered[zs, at + 1 : at + 2]
                value += phases[zs, 2] * gathered[zs, at + 2 : at + 3]
                high, low = split(value)
                upper[c * 64 : c * 64 + 32, d * CLUSTERS : (d + 1) * CLUSTERS] = high
                upper[c * 64 + 32 : c * 64 + 64, d * CLUSTERS : (d + 1) * CLUSTERS] = low
        total = mm_nt(upper[...], hot[zs])
        for c in range(3):
            plane = total[c * 64 : c * 64 + 32] + total[c * 64 + 32 : c * 64 + 64]
            for peer in range(WIDTH):
                sent1[peer, zs, c] = plane[peer * 8 : peer * 8 + 8]

        def send(j, carry):
            peer = x_peer(j)
            plane_copy(sent1.at[peer, zs], got1.at[x_index, zs], at_x(peer)).start()
            return carry

        lax.fori_loop(1, WIDTH, send, 0)

    build(z_index)

    def next_slab(i, carry):
        j = near_first(i)
        slab_copy(j).wait_recv()
        build(z_peer(DEPTH - j))
        return carry

    lax.fori_loop(1, DEPTH, next_slab, 0)
    got1[x_index] = sent1[x_index]

    def copy(stage, c, source, target, device):
        return pltpu.make_async_remote_copy(
            source,
            target,
            send_sem.at[stage, c],
            recv_sem.at[stage, c],
            device_id=device,
            device_id_type=MESH,
        )

    def to_all(stage, c, source, target, count, mine, peer_of, device_of):
        def one(j, carry):
            peer = peer_of(j)
            copy(stage, c, source.at[c, peer], target.at[c, mine], device_of(peer)).start()
            return carry

        lax.fori_loop(1, count, one, 0)
        target[c, mine] = source[c, mine]

    def whole(stage, c, source, target):
        peers = source.shape[1] - 1
        return copy(stage, c, source.at[c, pl.ds(0, peers)], target.at[c, pl.ds(0, peers)], at_row(1))

    def rows_of(k):
        return rows_table[k, 0], rows_table[k, 1]

    def lanes_of(k):
        return lanes_table[k, 0], lanes_table[k, 1]

    planes = plane_copy(sent1.at[pl.ds(0, WIDTH - 1)], got1.at[pl.ds(0, WIDTH - 1)], at_x(x_peer(1)))
    planes.wait_recv()

    def first_dimension(c, carry):
        values = forward(got1[:, :, c].reshape(G, G), *rows_of(1), *lanes_of(1), twiddle[2], twiddle[3])
        sent2[c] = values.reshape(COLS, 32, G)
        to_all(0, c, sent2, got2, COLS, col_index, col_peer, at_col)
        return carry

    lax.fori_loop(0, 3, first_dimension, 0)

    tile_copy.wait()
    near_sent[...] = jnp.zeros_like(near_sent)

    def slot(q, carry):
        charge = picked[q].astype(BF16)
        for b in range(3):
            total = mm(charge[0:1], blocks[q, 0, b])
            total += mm(charge[1:2], blocks[q, 1, b])
            total += mm(charge[2:3], blocks[q, 2, b])
            near_sent[q, b : b + 1] = total
        return carry

    lax.fori_loop(0, SLOTS, slot, 0)
    near_here[...] = near_sent[0:4]
    near_copies = []
    for side, j in ((0, ROWS - 1), (1, 1)):
        for k in range(4):
            near_copies.append(
                pltpu.make_async_remote_copy(
                    near_sent.at[4 + 2 * k + side],
                    near_got.at[2 * k + side],
                    near_sem.at[0, 2 * k + side],
                    near_sem.at[1, 2 * k + side],
                    device_id=at_row(j),
                    device_id_type=MESH,
                )
            )
    for near_copy in near_copies:
        near_copy.start()

    w1, w2, w3, inverse, weighting = screen(row_index, col_index)

    def second_dimension(c, carry):
        whole(0, c, sent2, got2).wait_recv()
        modes[c] = forward(got2[c].reshape(G, G), *rows_of(0), *lanes_of(0), twiddle[0], twiddle[1])
        return carry

    lax.fori_loop(0, 3, second_dimension, 0)

    inner = (w1 * modes[0] + w2 * modes[1] + w3 * modes[2]) * inverse
    for c, w in enumerate((w1, w2, w3)):
        modes[c] = (modes[c] - w * inner) * weighting

    def second_back(c, carry):
        values = backward(modes[c], *rows_of(3), *lanes_of(0), twiddle[0], twiddle[1])
        sent3[c] = values.reshape(COLS, 32, G)
        to_all(1, c, sent3, got3, COLS, col_index, col_peer, at_col)
        return carry

    lax.fori_loop(0, 3, second_back, 0)

    def first_back(c, carry):
        whole(1, c, sent3, got3).wait_recv()
        values = backward(got3[c].reshape(G, G), *rows_of(2), *lanes_of(1), twiddle[2], twiddle[3])
        sent4[c] = values.reshape(WIDTH, DEPTH, 8, G)
        to_all(2, c, sent4, got4, WIDTH, x_index, x_peer, at_x)
        return carry

    lax.fori_loop(0, 3, first_back, 0)
    sent5[...] = jnp.zeros_like(sent5)

    def sample(c, carry):
        whole(2, c, sent4, got4).wait_recv()

        def slab(zs, carry):
            high, low = split(got4[c, :, zs].reshape(32, G))
            both = mm(jnp.concatenate([high, low], axis=0), hot[zs])
            both = both[:32] + both[32:]
            for d in range(9):
                part = both[:, d * CLUSTERS : (d + 1) * CLUSTERS]
                for dz in range(3):
                    total = jnp.sum(part * phases[zs, dz], axis=0, keepdims=True)
                    sent5[c, zs, 3 * d + dz : 3 * d + dz + 1] = total
            return carry

        lax.fori_loop(0, DEPTH, slab, 0)
        to_all(3, c, sent5, got5, DEPTH, z_index, z_peer, at_z)
        return carry

    lax.fori_loop(0, 3, sample, 0)

    for near_copy in near_copies:
        near_copy.wait()

    def send_done(j, carry):
        slab_copy(j).wait_send()
        return carry

    lax.fori_loop(1, DEPTH, send_done, 0)
    planes.wait_send()

    def finish(c, carry):
        whole(0, c, sent2, got2).wait_send()
        whole(1, c, sent3, got3).wait_send()
        whole(2, c, sent4, got4).wait_send()
        whole(3, c, sent5, got5).wait()
        samples[c] = jnp.sum(got5[c], axis=0)
        return carry

    lax.fori_loop(0, 3, finish, 0)


def project_kernel(values, weight, near_here, near_got, landing, out):
    group = 8

    def clusters(i, carry):
        start = pl.multiple_of(i * group * PANELS, group * PANELS)
        block = weight[:, pl.ds(start, group * PANELS)]
        shift = lax.rem(CLUSTERS - i * group, CLUSTERS)
        for c in range(3):
            turned = pltpu.roll(values[c], shift, 1)
            for k in range(group):
                product = block[:, k * PANELS : (k + 1) * PANELS] * turned[:STENCIL, k : k + 1]
                place = pl.multiple_of(start + k * PANELS, PANELS)
                out[c : c + 1, pl.ds(place, PANELS)] = jnp.sum(product, axis=0, keepdims=True)
        return carry

    lax.fori_loop(0, CLUSTERS // group, clusters, 0)
    for q in range(SLOTS):
        place = pl.multiple_of(landing[q] * PANELS, PANELS)
        arrived = near_here[q] if q < 4 else near_got[q - 4]
        out[:, pl.ds(place, PANELS)] += arrived[:3]


VMEM = pl.BlockSpec(memory_space=pltpu.VMEM)
SMEM = pl.BlockSpec(memory_space=pltpu.SMEM)
ANY = pl.BlockSpec(memory_space=pl.ANY)
LIMIT = 48 * 1024 * 1024


def shape(dims, dtype=F32):
    return jax.ShapeDtypeStruct(dims, dtype)


def per_device(
    density, interp_weight, proj_weight, stencil_corner, near_tiles, pair_target, pair_landing, pair_count
):
    line, rows_table, lanes_table, twiddle = (jnp.asarray(t) for t in make_tables())
    packed, picked = pl.pallas_call(
        spread_kernel,
        out_shape=(shape((PACKED, CLUSTERS)), shape((SLOTS, 8, PANELS))),
        in_specs=[VMEM] * 3 + [SMEM] * 2,
        out_specs=(VMEM, VMEM),
        compiler_params=pltpu.CompilerParams(vmem_limit_bytes=LIMIT),
    )(density, interp_weight, stencil_corner, pair_target, pair_count)
    planes, by_cols = (WIDTH, DEPTH, 3, 8, G), (3, COLS, 32, G)
    by_width, by_depth = (3, WIDTH, DEPTH, 8, G), (3, DEPTH, 32, CLUSTERS)
    samples, near_here, near_got = pl.pallas_call(
        exchange_kernel,
        out_shape=(shape((3, 32, CLUSTERS)), shape((4, 8, PANELS)), shape((8, 8, PANELS))),
        in_specs=[VMEM] * 6 + [ANY],
        out_specs=(VMEM, VMEM, VMEM),
        scratch_shapes=[
            pltpu.VMEM((DEPTH, PACKED, CLUSTERS), F32),
            pltpu.VMEM((DEPTH, G, 9 * CLUSTERS), BF16),
            pltpu.VMEM((DEPTH, 3, 32, CLUSTERS), F32),
            pltpu.VMEM((192, 9 * CLUSTERS), BF16),
            pltpu.VMEM(planes, F32),
            pltpu.VMEM(planes, F32),
            pltpu.VMEM(by_cols, F32),
            pltpu.VMEM(by_cols, F32),
            pltpu.VMEM((3, G, G), F32),
            pltpu.VMEM(by_cols, F32),
            pltpu.VMEM(by_cols, F32),
            pltpu.VMEM(by_width, F32),
            pltpu.VMEM(by_width, F32),
            pltpu.VMEM(by_depth, F32),
            pltpu.VMEM(by_depth, F32),
            pltpu.VMEM((SLOTS, 8, PANELS), F32),
            pltpu.VMEM((SLOTS, 3, 3, PANELS, PANELS), BF16),
            pltpu.SemaphoreType.DMA((DEPTH,)),
            pltpu.SemaphoreType.DMA((DEPTH,)),
            pltpu.SemaphoreType.DMA((2,)),
            pltpu.SemaphoreType.DMA((4, 3)),
            pltpu.SemaphoreType.DMA((4, 3)),
            pltpu.SemaphoreType.DMA((2, 8)),
            pltpu.SemaphoreType.DMA,
        ],
        compiler_params=pltpu.CompilerParams(
            vmem_limit_bytes=LIMIT, collective_id=0, has_side_effects=True
        ),
    )(packed, line, rows_table, lanes_table, twiddle, picked, near_tiles)
    return pl.pallas_call(
        project_kernel,
        out_shape=shape((3, CLUSTERS * PANELS)),
        in_specs=[VMEM] * 4 + [SMEM],
        out_specs=VMEM,
        compiler_params=pltpu.CompilerParams(vmem_limit_bytes=LIMIT),
    )(samples, proj_weight, near_here, near_got, pair_landing)


def solution(mesh):
    flat = P(None, ("row", "col"))
    slots = P(("row", "col"))
    in_specs = (flat, flat, flat, flat, P(("row", "col"), None, None, None, None), slots, slots, slots)
    return jax.shard_map(
        per_device, mesh=mesh, in_specs=in_specs, out_specs=flat, check_vma=False
    )
```

time: 89.5 us -> 78.9 us (0.88)
  Pallas kernels: 82.4 us -> 72.8 us
  local copies, waits for them, and re-layouts: 6.05 us -> 5.11 us
    pallas_call x2, Pallas kernels: 73.9 us -> 65.9 us  [the longest x1 62.4 us: per_device(): pl.pallas_call(exchange_kernel, out_shape=(shape((3, 32, CLUSTERS)), shap...]
    pallas_call x1, Pallas kernels: 8.51 us -> 6.95 us  [per_device(): pl.pallas_call(project_kernel, out_shape=shape((3, CLUSTERS * PANELS)), i...]
    unnamed x20, local copies, waits for them, and re-layouts: 6.05 us -> 5.11 us
where the time goes in v1:
time: 78.9 us; the launch traced here: 78.7 us
  Pallas kernels  72.8 us (92%)
  local copies, waits for them, and re-layouts  5.11 us (6%)
    pallas_call x1, Pallas kernels, per_device(): pl.pallas_call(exchange_kernel, out_shape=(shape((3, 32, CLUSTERS)), shap...  62.4 us
    pallas_call x1, Pallas kernels, per_device(): pl.pallas_call(project_kernel, out_shape=shape((3, CLUSTERS * PANELS)), i...  6.95 us
    unnamed x20, local copies, waits for them, and re-layouts  5.11 us
    pallas_call x1, Pallas kernels, per_device(): pl.pallas_call(spread_kernel, out_shape=(shape((PACKED, CLUSTERS)), shape...  3.45 us

profile of v1, /device:TPU:1, one launch (start us, length us, event | category | flops | bytes accessed | tf_op | source)
XLA Modules:
  0.0 78.7 jit_solution(1390642338497564538)
XLA Ops:
  0.7 0.0 copy-start
  0.7 1.6 %copy-done = f32[27,16384]{1,0:T(8,128)S(1)} copy-done((f32[27,16384]{1,0:T(8,128)S(1)}, f32[27,16384]{1,0:T(8,128)}, u32[]{:S(2)}) %copy-start) | copy-done | bytes 1769496
  2.2 0.0 copy-start.5
  2.2 0.9 %copy-done.5 = f32[3,16384]{1,0:T(4,128)S(1)} copy-done((f32[3,16384]{1,0:T(4,128)S(1)}, f32[3,16384]{1,0:T(4,128)}, u32[]{:S(2)}) %copy-start.5) | copy-done | bytes 196632
  3.2 0.0 copy-start.7
  3.2 0.7 copy-done.7
  3.9 0.0 copy-start.8
  3.9 0.7 copy-done.8
  4.5 0.0 copy-start.2
  4.5 0.0 copy-start.3
  4.5 0.0 copy-start.6
  4.5 3.4 %shard_map.118 = (f32[88,128]{1,0:T(8,128)S(1)}, f32[12,8,128]{2,1,0:T(8,128)S(1)}) custom-call(f32[3,16384]{1,0:T(4,128)S(1)} %copy-done.5, f32[27,16384]{1,0:T(8,128)S(1)} %copy-done, s32[3,128]{1,0:T(4,128)S(1)} %copy-done.7, s32[12]{0:T(128)S(1)} %copy-done.8, s32[1]{0:T(128)S(6)} %copy.13.count), custom_call_target="tpu_custom_call" | custom-call | tf_op jit(solution)/shard_map/pallas_call | solution.py:477
  8.0 0.0 copy-done.2
  8.0 0.0 copy-done.3
  8.0 0.0 copy-done.6
  8.0 0.0 copy-start.4
  8.0 1.2 %copy-done.4 = bf16[4,2,256,256]{3,2,1,0:T(8,128)(2,1)S(1)} copy-done((bf16[4,2,256,256]{3,2,1,0:T(8,128)(2,1)S(1)}, bf16[4,2,256,256]{3,2,1,0:T(8,128)(2,1)}, u32[]{:S(2)}) %copy-start.4) | copy-done | bytes 1048600
  9.3 0.0 copy-start.1
  9.3 0.0 copy-start.9
  9.3 62.4 %shard_map.119 = (f32[3,32,128]{2,1,0:T(8,128)S(1)}, f32[4,8,128]{2,1,0:T(8,128)S(1)}, f32[8,8,128]{2,1,0:T(8,128)S(1)}) custom-call(f32[88,128]{1,0:T(8,128)S(1)} %get-tuple-element.10.packed, bf16[8,64,256]{2,1,0:T(8,128)(2,1)S(1)} %copy-done.6, bf16[4,2,256,256]{3,2,1,0:T(8,128)(2,1)S(1)} %copy-done.4, bf16[2,2,256,512]{3,2,1,0:T(8,128)(2,1)S(1)} %copy-done.3, ...), custom_call_target="tpu_custom_call" | custom-call | tf_op jit(solution)/shard_map/pallas_call | solution.py:486
  71.7 0.0 copy-done.1
  71.7 0.0 copy-done.9
  71.7 7.0 %shard_map.120 = f32[3,16384]{1,0:T(4,128)} custom-call(f32[3,32,128]{2,1,0:T(8,128)S(1)} %get-tuple-element.12.values, f32[27,16384]{1,0:T(8,128)S(1)} %copy-done.1, f32[4,8,128]{2,1,0:T(8,128)S(1)} %get-tuple-element.13.near_here, f32[8,8,128]{2,1,0:T(8,128)S(1)} %get-tuple-element.14.near_got, s32[12]{0:T(128)S(1)} %copy-done.9), custom_call_target="tpu_custom_call" | custom-call | tf_op jit(solution)/shard_map/pallas_call | solution.py:521
Async XLA Ops:
  0.7 1.6 %copy-start = (f32[27,16384]{1,0:T(8,128)S(1)}, f32[27,16384]{1,0:T(8,128)}, u32[]{:S(2)}) copy-start(f32[27,16384]{1,0:T(8,128)} %weight.2) | copy-start | bytes 5308420
  2.2 0.9 %copy-start.5 = (f32[3,16384]{1,0:T(4,128)S(1)}, f32[3,16384]{1,0:T(4,128)}, u32[]{:S(2)}) copy-start(f32[3,16384]{1,0:T(4,128)} %density.1) | copy-start | bytes 589828
  3.2 0.7 copy-start.7
  3.9 0.7 copy-start.8
  4.5 3.5 %copy-start.2 = (f32[4,256,256]{2,1,0:T(8,128)S(1)}, f32[4,256,256]{2,1,0:T(8,128)}, u32[]{:S(2)}) copy-start(f32[4,256,256]{2,1,0:T(8,128)} %constant.11.clone.twiddle) | copy-start | bytes 3145732
  4.5 3.5 %copy-start.3 = (bf16[2,2,256,512]{3,2,1,0:T(8,128)(2,1)S(1)}, bf16[2,2,256,512]{3,2,1,0:T(8,128)(2,1)}, u32[]{:S(2)}) copy-start(bf16[2,2,256,512]{3,2,1,0:T(8,128)(2,1)} %constant.10.clone.lanes_table) | copy-start | bytes 3145732
  4.5 3.5 %copy-start.6 = (bf16[8,64,256]{2,1,0:T(8,128)(2,1)S(1)}, bf16[8,64,256]{2,1,0:T(8,128)(2,1)}, u32[]{:S(2)}) copy-start(bf16[8,64,256]{2,1,0:T(8,128)(2,1)} %constant.8.clone.line) | copy-start | bytes 786436
  8.0 1.2 %copy-start.4 = (bf16[4,2,256,256]{3,2,1,0:T(8,128)(2,1)S(1)}, bf16[4,2,256,256]{3,2,1,0:T(8,128)(2,1)}, u32[]{:S(2)}) copy-start(bf16[4,2,256,256]{3,2,1,0:T(8,128)(2,1)} %constant.9.clone.rows_table) | copy-start | bytes 3145732
  9.3 62.5 %copy-start.1 = (f32[27,16384]{1,0:T(8,128)S(1)}, f32[27,16384]{1,0:T(8,128)}, u32[]{:S(2)}) copy-start(f32[27,16384]{1,0:T(8,128)} %weight.3) | copy-start | bytes 5308420
  9.3 62.5 %copy-start.9 = (s32[12]{0:T(128)S(1)}, s32[12]{0:T(128)}, u32[]{:S(2)}) copy-start(s32[12]{0:T(128)} %landing.1) | copy-start | bytes 148

commit v2 on v1

--- a/solution.py
+++ b/solution.py
@@ -16,6 +16,8 @@
 DEPTH = 8
 WIDTH = 4
 PACKED = 88
+PIECES = 4
+GROUP = 8
 CLUSTERS = 128
 PANELS = 128
 SLOTS = 12
@@ -134,12 +136,11 @@
     return w1, w2, w3, 1.0 / jnp.maximum(squared, 1.0), kept * fold / (squared + 0.5)
 
 
-def spread_kernel(density, weight, corner, target, count, packed, picked):
-    row_index, col_index = lax.axis_index("row"), lax.axis_index("col")
+def spread(weight, density, first, sums):
     lane = lax.broadcasted_iota(jnp.int32, (STENCIL, CLUSTERS), 1)
     group = 8
 
-    def gather_sums(i, sums):
+    def some(i, sums):
         start = pl.multiple_of(i * group * PANELS, group * PANELS)
         block = weight[:, pl.ds(start, group * PANELS)]
         charge = density[:, pl.ds(start, group * PANELS)]
@@ -151,35 +152,43 @@
                 sums[c] = jnp.where(lane == i * group + k, total, sums[c])
         return tuple(sums)
 
-    picked[...] = jnp.zeros_like(picked)
-    live = count[0]
-    for q in range(SLOTS):
-        start = pl.multiple_of(target[q] * PANELS, PANELS)
-        charge = density[:, pl.ds(start, PANELS)].astype(BF16).astype(F32)
-        picked[q, 0:3] = jnp.where(q < live, charge, jnp.zeros_like(charge))
-
-    zero = jnp.zeros((STENCIL, CLUSTERS), F32)
-    sums = lax.fori_loop(0, CLUSTERS // group, gather_sums, (zero,) * 3)
-
-    corners = corner[...]
-    local = (corners[0:1] - row_index * 8) * 32 + (corners[1:2] - col_index * 32)
-    packed[80:PACKED] = jnp.zeros((PACKED - 80, CLUSTERS), F32)
-    for c in range(3):
-        packed[c * STENCIL : (c + 1) * STENCIL] = sums[c]
-    packed[81:82] = local.astype(F32)
-    packed[82:83] = corners[2:3].astype(F32)
-
-
-def exchange_kernel(
-    packed, line, rows_table, lanes_table, twiddle, picked, tiles,
-    samples, near_here, near_got,
-    gathered, hot, phases, upper, sent1, got1, sent2, got2, modes, sent3, got3, sent4, got4, sent5, got5, near_sent, blocks,
-    slab_send, slab_recv, plane_sem, send_sem, recv_sem, near_sem, tile_sem,
+    groups = CLUSTERS // PIECES // group
+    return lax.fori_loop(first * groups, (first + 1) * groups, some, sums)
+
+
+def whole_kernel(
+    corner, target, landing, count, density_in, interp_in, proj_in, line_in, rows_in, lanes_in, twiddle_in, tiles_in,
+    out,
+    density, interp, proj, line, rows_table, lanes_table, twiddle, blocks,
+    packed, picked, gathered, hot, phases, upper, sent1, got1, sent2, got2, modes, sent3, got3, sent4, got4, sent5, got5,
+    near_sent, near_got, near_rows, near_term, proj_high, proj_low, values,
+    load_sem, slab_send, slab_recv, plane_sem, send_sem, recv_sem, near_sem,
 ):
     row_index, col_index = lax.axis_index("row"), lax.axis_index("col")
     z_index, x_index = row_index // WIDTH, lax.rem(row_index, WIDTH)
-    tile_copy = pltpu.make_async_copy(tiles, blocks, tile_sem)
-    tile_copy.start()
+    width = CLUSTERS * PANELS // PIECES
+
+    def piece(k):
+        at = pl.ds(k * width, width)
+        return pltpu.make_async_copy(interp_in.at[:, at], interp.at[:, at], load_sem.at[k])
+
+    loads = [
+        pltpu.make_async_copy(source, target_ref, load_sem.at[PIECES + k])
+        for k, (source, target_ref) in enumerate(
+            (
+                (density_in, density),
+                (line_in, line),
+                (rows_in, rows_table),
+                (lanes_in, lanes_table),
+                (twiddle_in, twiddle),
+                (tiles_in, blocks),
+                (proj_in, proj),
+            )
+        )
+    ]
+    loads[0].start()
+    for k in range(PIECES):
+        piece(k).start()
 
     def z_peer(j):
         return lax.rem(z_index + j, DEPTH)
@@ -224,6 +233,20 @@
     lax.fori_loop(1, COLS, greet_col, 0)
     greet(at_row(1))
     greet(at_row(ROWS - 1))
+    loads[0].wait()
+    sums = (jnp.zeros((STENCIL, CLUSTERS), F32),) * 3
+    for k in range(PIECES):
+        piece(k).wait()
+        if k == 0:
+            for load in loads[1:]:
+                load.start()
+        sums = spread(interp, density, k, sums)
+    corners = corner[...]
+    packed[80:PACKED] = jnp.zeros((PACKED - 80, CLUSTERS), F32)
+    for c in range(3):
+        packed[c * STENCIL : (c + 1) * STENCIL] = sums[c]
+    packed[81:82] = ((corners[0:1] - row_index * 8) * 32 + (corners[1:2] - col_index * 32)).astype(F32)
+    packed[82:83] = corners[2:3].astype(F32)
     pl.semaphore_wait(barrier, DEPTH + WIDTH + COLS - 3 + 2)
 
     def near_first(i):
@@ -285,6 +308,7 @@
 
         lax.fori_loop(1, WIDTH, send, 0)
 
+    loads[1].wait()
     build(z_index)
 
     def next_slab(i, carry):
@@ -326,6 +350,8 @@
         return lanes_table[k, 0], lanes_table[k, 1]
 
     planes = plane_copy(sent1.at[pl.ds(0, WIDTH - 1)], got1.at[pl.ds(0, WIDTH - 1)], at_x(x_peer(1)))
+    for load in loads[2:5]:
+        load.wait()
     planes.wait_recv()
 
     def first_dimension(c, carry):
@@ -336,8 +362,27 @@
 
     lax.fori_loop(0, 3, first_dimension, 0)
 
-    tile_copy.wait()
+    loads[5].wait()
     near_sent[...] = jnp.zeros_like(near_sent)
+    picked[...] = jnp.zeros_like(picked)
+    nobody = jnp.full((3, PANELS), -1, jnp.int32)
+    wanted = [
+        jnp.where(jnp.full((3, PANELS), q, jnp.int32) < count[0], jnp.full((3, PANELS), target[q], jnp.int32), nobody)
+        for q in range(SLOTS)
+    ]
+
+    def pick(i, charges):
+        charges = list(charges)
+        for k in range(GROUP):
+            cluster = i * GROUP + k
+            charge = density[:, pl.ds(pl.multiple_of(cluster * PANELS, PANELS), PANELS)]
+            for q in range(SLOTS):
+                charges[q] = jnp.where(wanted[q] == cluster, charge, charges[q])
+        return tuple(charges)
+
+    charges = lax.fori_loop(0, CLUSTERS // GROUP, pick, (jnp.zeros((3, PANELS), F32),) * SLOTS)
+    for q in range(SLOTS):
+        picked[q, 0:3] = charges[q]
 
     def slot(q, carry):
         charge = picked[q].astype(BF16)
@@ -349,7 +394,6 @@
         return carry
 
     lax.fori_loop(0, SLOTS, slot, 0)
-    near_here[...] = near_sent[0:4]
     near_copies = []
     for side, j in ((0, ROWS - 1), (1, 1)):
         for k in range(4):
@@ -366,6 +410,20 @@
     for near_copy in near_copies:
         near_copy.start()
 
+    loads[6].wait()
+    below = jnp.zeros((32 - STENCIL, PANELS), F32)
+
+    def halve(i, carry):
+        start = pl.multiple_of(i * GROUP * PANELS, GROUP * PANELS)
+        for k in range(GROUP):
+            block = proj[:, pl.ds(start + k * PANELS, PANELS)]
+            high, low = split(jnp.concatenate([block, below], axis=0))
+            proj_high[i, k * 32 : (k + 1) * 32] = high
+            proj_low[i, k * 32 : (k + 1) * 32] = low
+        return carry
+
+    lax.fori_loop(0, CLUSTERS // GROUP, halve, 0)
+
     w1, w2, w3, inverse, weighting = screen(row_index, col_index)
 
     def second_dimension(c, carry):
@@ -396,6 +454,21 @@
 
     lax.fori_loop(0, 3, first_back, 0)
     sent5[...] = jnp.zeros_like(sent5)
+
+    for near_copy in near_copies:
+        near_copy.wait()
+    near_rows[...] = jnp.zeros_like(near_rows)
+    row = lax.broadcasted_iota(jnp.int32, (CLUSTERS, CLUSTERS), 0)
+    lane = lax.broadcasted_iota(jnp.int32, (CLUSTERS, CLUSTERS), 1)
+    lands = jnp.zeros((CLUSTERS, CLUSTERS), F32)
+    for q in range(SLOTS):
+        lands = jnp.where((lane == q) & (row == landing[q]), 1.0, lands)
+        for b in range(3):
+            arrived = near_sent[q, b : b + 1] if q < 4 else near_got[q - 4, b : b + 1]
+            near_rows[q : q + 1, b * PANELS : (b + 1) * PANELS] = arrived
+    lands = lands.astype(BF16)
+    high, low = split(near_rows[...])
+    near_term[...] = mm(lands, high) + mm(lands, low)
 
     def sample(c, carry):
         whole(2, c, sent4, got4).wait_recv()
@@ -417,9 +490,6 @@
 
     lax.fori_loop(0, 3, sample, 0)
 
-    for near_copy in near_copies:
-        near_copy.wait()
-
     def send_done(j, carry):
         slab_copy(j).wait_send()
         return carry
@@ -432,38 +502,38 @@
         whole(1, c, sent3, got3).wait_send()
         whole(2, c, sent4, got4).wait_send()
         whole(3, c, sent5, got5).wait()
-        samples[c] = jnp.sum(got5[c], axis=0)
-        return carry
-
+        total = jnp.sum(got5[c], axis=0)
+        turned = jnp.concatenate([total] * 4, axis=0).T
+        both = jnp.concatenate([turned, turned], axis=1)
+        both = jnp.where(own, both, jnp.zeros_like(both))
+        high = both.astype(BF16).astype(F32)
+        low = both - high
+        for i in range(CLUSTERS // GROUP):
+            at = slice(i * GROUP, (i + 1) * GROUP)
+            values[i, c] = jnp.concatenate([high[at], low[at]], axis=0).astype(BF16)
+        return carry
+
+    own = (lax.broadcasted_iota(jnp.int32, (CLUSTERS, G), 0) & (GROUP - 1)) == (
+        lax.broadcasted_iota(jnp.int32, (CLUSTERS, G), 1) >> 5
+    )
     lax.fori_loop(0, 3, finish, 0)
 
-
-def project_kernel(values, weight, near_here, near_got, landing, out):
-    group = 8
-
-    def clusters(i, carry):
-        start = pl.multiple_of(i * group * PANELS, group * PANELS)
-        block = weight[:, pl.ds(start, group * PANELS)]
-        shift = lax.rem(CLUSTERS - i * group, CLUSTERS)
+    def project(i, carry):
+        point_values = values[i].reshape(3 * 2 * GROUP, G)
+        both = mm(point_values, proj_high[i]) + mm(point_values, proj_low[i])
+        at = pl.ds(pl.multiple_of(i * GROUP, GROUP), GROUP)
         for c in range(3):
-            turned = pltpu.roll(values[c], shift, 1)
-            for k in range(group):
-                product = block[:, k * PANELS : (k + 1) * PANELS] * turned[:STENCIL, k : k + 1]
-                place = pl.multiple_of(start + k * PANELS, PANELS)
-                out[c : c + 1, pl.ds(place, PANELS)] = jnp.sum(product, axis=0, keepdims=True)
-        return carry
-
-    lax.fori_loop(0, CLUSTERS // group, clusters, 0)
-    for q in range(SLOTS):
-        place = pl.multiple_of(landing[q] * PANELS, PANELS)
-        arrived = near_here[q] if q < 4 else near_got[q - 4]
-        out[:, pl.ds(place, PANELS)] += arrived[:3]
+            far = both[c * 2 * GROUP : c * 2 * GROUP + GROUP] + both[c * 2 * GROUP + GROUP : (c + 1) * 2 * GROUP]
+            out[c, at] = far + near_term[at, c * PANELS : (c + 1) * PANELS]
+        return carry
+
+    lax.fori_loop(0, CLUSTERS // GROUP, project, 0)
 
 
 VMEM = pl.BlockSpec(memory_space=pltpu.VMEM)
 SMEM = pl.BlockSpec(memory_space=pltpu.SMEM)
 ANY = pl.BlockSpec(memory_space=pl.ANY)
-LIMIT = 48 * 1024 * 1024
+LIMIT = 60 * 1024 * 1024
 
 
 def shape(dims, dtype=F32):
@@ -474,21 +544,19 @@
     density, interp_weight, proj_weight, stencil_corner, near_tiles, pair_target, pair_landing, pair_count
 ):
     line, rows_table, lanes_table, twiddle = (jnp.asarray(t) for t in make_tables())
-    packed, picked = pl.pallas_call(
-        spread_kernel,
-        out_shape=(shape((PACKED, CLUSTERS)), shape((SLOTS, 8, PANELS))),
-        in_specs=[VMEM] * 3 + [SMEM] * 2,
-        out_specs=(VMEM, VMEM),
-        compiler_params=pltpu.CompilerParams(vmem_limit_bytes=LIMIT),
-    )(density, interp_weight, stencil_corner, pair_target, pair_count)
     planes, by_cols = (WIDTH, DEPTH, 3, 8, G), (3, COLS, 32, G)
     by_width, by_depth = (3, WIDTH, DEPTH, 8, G), (3, DEPTH, 32, CLUSTERS)
-    samples, near_here, near_got = pl.pallas_call(
-        exchange_kernel,
-        out_shape=(shape((3, 32, CLUSTERS)), shape((4, 8, PANELS)), shape((8, 8, PANELS))),
-        in_specs=[VMEM] * 6 + [ANY],
-        out_specs=(VMEM, VMEM, VMEM),
+    held = (density, interp_weight, proj_weight, line, rows_table, lanes_table, twiddle, near_tiles)
+    weights = pltpu.VMEM((CLUSTERS // GROUP, G, PANELS), BF16)
+    out = pl.pallas_call(
+        whole_kernel,
+        out_shape=shape((3, CLUSTERS, PANELS)),
+        in_specs=[VMEM] + [SMEM] * 3 + [ANY] * 8,
+        out_specs=VMEM,
         scratch_shapes=[
+            *(pltpu.VMEM(array.shape, array.dtype) for array in held),
+            pltpu.VMEM((PACKED, CLUSTERS), F32),
+            pltpu.VMEM((SLOTS, 8, PANELS), F32),
             pltpu.VMEM((DEPTH, PACKED, CLUSTERS), F32),
             pltpu.VMEM((DEPTH, G, 9 * CLUSTERS), BF16),
             pltpu.VMEM((DEPTH, 3, 32, CLUSTERS), F32),
@@ -505,26 +573,25 @@
             pltpu.VMEM(by_depth, F32),
             pltpu.VMEM(by_depth, F32),
             pltpu.VMEM((SLOTS, 8, PANELS), F32),
-            pltpu.VMEM((SLOTS, 3, 3, PANELS, PANELS), BF16),
+            pltpu.VMEM((8, 8, PANELS), F32),
+            pltpu.VMEM((CLUSTERS, 3 * PANELS), F32),
+            pltpu.VMEM((CLUSTERS, 3 * PANELS), F32),
+            weights,
+            weights,
+            pltpu.VMEM((CLUSTERS // GROUP, 3, 2 * GROUP, G), BF16),
+            pltpu.SemaphoreType.DMA((PIECES + 7,)),
             pltpu.SemaphoreType.DMA((DEPTH,)),
             pltpu.SemaphoreType.DMA((DEPTH,)),
             pltpu.SemaphoreType.DMA((2,)),
             pltpu.SemaphoreType.DMA((4, 3)),
             pltpu.SemaphoreType.DMA((4, 3)),
             pltpu.SemaphoreType.DMA((2, 8)),
-            pltpu.SemaphoreType.DMA,
         ],
         compiler_params=pltpu.CompilerParams(
             vmem_limit_bytes=LIMIT, collective_id=0, has_side_effects=True
         ),
-    )(packed, line, rows_table, lanes_table, twiddle, picked, near_tiles)
-    return pl.pallas_call(
-        project_kernel,
-        out_shape=shape((3, CLUSTERS * PANELS)),
-        in_specs=[VMEM] * 4 + [SMEM],
-        out_specs=VMEM,
-        compiler_params=pltpu.CompilerParams(vmem_limit_bytes=LIMIT),
-    )(samples, proj_weight, near_here, near_got, pair_landing)
+    )(stencil_corner, pair_target, pair_landing, pair_count, *held)
+    return out.reshape(3, CLUSTERS * PANELS)
 
 
 def solution(mesh):

time: 78.9 us -> 71.2 us (0.902)
  Pallas kernels: 72.8 us -> 68.6 us
  local copies, waits for them, and re-layouts: 5.11 us -> 1.77 us
    pallas_call x3 -> x1, Pallas kernels: 72.8 us -> 68.6 us  [per_device(): pl.pallas_call(whole_kernel, out_shape=shape((3, CLUSTERS, PANELS)), in_s...]
    unnamed x20 -> x1, local copies, waits for them, and re-layouts: 5.11 us -> 1.77 us
where the time goes in v2:
time: 71.2 us; the launch traced here: 71 us
  Pallas kernels  68.6 us (96%)
  local copies, waits for them, and re-layouts  1.77 us (2%)
    pallas_call x1, Pallas kernels, per_device(): pl.pallas_call(whole_kernel, out_shape=shape((3, CLUSTERS, PANELS)), in_s...  68.6 us
    unnamed x1, local copies, waits for them, and re-layouts  1.77 us

profile of v2, /device:TPU:1, one launch (start us, length us, event | category | flops | bytes accessed | tf_op | source)
XLA Modules:
  0.0 71.0 jit_solution(7223672065640836187)
XLA Ops:
  0.7 68.6 %shard_map.118 = f32[3,128,128]{2,1,0:T(8,128)} custom-call(s32[3,128]{1,0:T(4,128)} %corner.1, s32[12]{0:T(128)} %target.1, s32[12]{0:T(128)} %landing.1, s32[1]{0:T(128)S(6)} %copy.16.count, f32[3,16384]{1,0:T(4,128)} %density_in.1, f32[27,16384]{1,0:T(8,128)} %interp_in.1, f32[27,16384]{1,0:T(8,128)} %proj_in.1, ...), custom_call_target="tpu_custom_call" | custom-call | tf_op jit(solution)/shard_map/pallas_call | solution.py:551
  69.3 1.8 %copy.15 = f32[1,3,128,128]{3,1,2,0:T(4,128)} copy(f32[1,3,128,128]{3,2,1,0:T(8,128)} %bitcast.4) | data formatting | bytes 393216

commit v3 on v2

--- a/solution.py
+++ b/solution.py
@@ -46,6 +46,9 @@
     line = np.stack([np.cos(theta), -np.sin(theta)]).reshape(2, DEPTH, WIDTH, 4, G)
     line = line.transpose(1, 2, 0, 3, 4).reshape(DEPTH, 32, G)
     line = halves(line).transpose(1, 0, 2, 3).reshape(DEPTH, 64, G)
+    step = 2 * np.pi * np.arange(128).reshape(DEPTH, WIDTH, 1, 4) / G
+    onward = np.stack([np.cos(step) + np.zeros((2, 1)), np.sin(step) * np.array([[1.0], [-1.0]])], axis=1)
+    onward = np.broadcast_to(onward.reshape(DEPTH, 2, 32, 1), (DEPTH, 2, 32, CLUSTERS)).astype(np.float32)
     eight = np.arange(8)
     wide = np.arange(32)
     turn8 = rotation(two_pi * (eight[:, None] * eight[None, :] % 8) / 8)
@@ -65,7 +68,7 @@
     ).astype(np.float32)
     rows_table = np.stack([halves(t) for t in (second, first, first.T, second.T)])
     lanes_table = np.stack([halves(np.concatenate(t, axis=1)) for t in (lane32, lane8)])
-    return line, rows_table, lanes_table, twiddle
+    return line, np.ascontiguousarray(onward), rows_table, lanes_table, twiddle
 
 
 def split(values):
@@ -82,7 +85,7 @@
 
 
 def swap(values):
-    grouped = values.reshape(32, 8, values.shape[1])
+    grouped = values.reshape(values.shape[0] // 8, 8, values.shape[1])
     return pltpu.roll(grouped, 4, 1).reshape(values.shape)
 
 
@@ -153,13 +156,13 @@
         return tuple(sums)
 
     groups = CLUSTERS // PIECES // group
-    return lax.fori_loop(first * groups, (first + 1) * groups, some, sums)
+    return lax.fori_loop(first * groups, (first + 1) * groups, some, sums, unroll=4)
 
 
 def whole_kernel(
-    corner, target, landing, count, density_in, interp_in, proj_in, line_in, rows_in, lanes_in, twiddle_in, tiles_in,
+    corner, target, landing, count, density_in, interp_in, proj_in, line_in, onward_in, rows_in, lanes_in, twiddle_in, tiles_in,
     out,
-    density, interp, proj, line, rows_table, lanes_table, twiddle, blocks,
+    density, interp, proj, line, onward, rows_table, lanes_table, twiddle, blocks,
     packed, picked, gathered, hot, phases, upper, sent1, got1, sent2, got2, modes, sent3, got3, sent4, got4, sent5, got5,
     near_sent, near_got, near_rows, near_term, proj_high, proj_low, values,
     load_sem, slab_send, slab_recv, plane_sem, send_sem, recv_sem, near_sem,
@@ -178,6 +181,7 @@
             (
                 (density_in, density),
                 (line_in, line),
+                (onward_in, onward),
                 (rows_in, rows_table),
                 (lanes_in, lanes_table),
                 (twiddle_in, twiddle),
@@ -249,25 +253,22 @@
     packed[82:83] = corners[2:3].astype(F32)
     pl.semaphore_wait(barrier, DEPTH + WIDTH + COLS - 3 + 2)
 
-    def near_first(i):
+    def distance(i):
         odd = lax.rem(i, 2)
-        return odd * ((i + 1) // 2) + (1 - odd) * (DEPTH - i // 2)
-
-    def slab_copy(j):
+        return odd * (DEPTH - (i + 1) // 2) + (1 - odd) * (i // 2)
+
+    def slab_copy(i):
         return pltpu.make_async_remote_copy(
             packed,
             gathered.at[z_index],
-            slab_send.at[j],
-            slab_recv.at[j],
-            device_id=at_z(z_peer(j)),
+            slab_send.at[i],
+            slab_recv.at[i],
+            device_id=at_z(z_peer(DEPTH - distance(i))),
             device_id_type=MESH,
         )
 
-    def send_slab(i, carry):
-        slab_copy(near_first(i)).start()
-        return carry
-
-    lax.fori_loop(1, DEPTH, send_slab, 0)
+    slab_copy(1).start()
+    slab_copy(2).start()
     gathered[z_index] = packed[...]
 
     def plane_copy(source, target, device):
@@ -279,25 +280,34 @@
 
     def build(zs):
         local, depth = gathered[zs, 81:82], gathered[zs, 82:83]
+        at = jnp.where(cell == depth, 1.0, 0.0).astype(BF16)
+        both = mm(line[z_index], at)
+        turn = [both[:32] + both[32:]]
+        for dz in range(1, 3):
+            turn.append(turn[-1] * onward[z_index, 0] + swap(turn[-1]) * onward[z_index, 1])
         for dz in range(3):
-            at = jnp.where(cell == depth + float(dz), 1.0, 0.0).astype(BF16)
-            both = mm(line[z_index], at)
-            phases[zs, dz] = both[:32] + both[32:]
-        for d in range(9):
-            here = jnp.where(cell == local + float(d // 3 * 32 + d % 3), 1.0, 0.0).astype(BF16)
-            hot[zs, :, d * CLUSTERS : (d + 1) * CLUSTERS] = here
-        for c in range(3):
-            for d in range(9):
-                at = c * STENCIL + 3 * d
-                value = phases[zs, 0] * gathered[zs, at : at + 1]
-                value += phases[zs, 1] * gathered[zs, at + 1 : at + 2]
-                value += phases[zs, 2] * gathered[zs, at + 2 : at + 3]
-                high, low = split(value)
-                upper[c * 64 : c * 64 + 32, d * CLUSTERS : (d + 1) * CLUSTERS] = high
-                upper[c * 64 + 32 : c * 64 + 64, d * CLUSTERS : (d + 1) * CLUSTERS] = low
+            phases[zs, dz] = turn[dz]
+        for dy in range(3):
+            here = jnp.where(cell == local + float(dy), 1.0, 0.0).astype(BF16)
+            hot[zs, :, dy * CLUSTERS : (dy + 1) * CLUSTERS] = here
+        for dx in range(3):
+            for c in range(3):
+                for dy in range(3):
+                    at = c * STENCIL + 9 * dx + 3 * dy
+                    value = turn[0] * gathered[zs, at : at + 1]
+                    value += turn[1] * gathered[zs, at + 1 : at + 2]
+                    value += turn[2] * gathered[zs, at + 2 : at + 3]
+                    high, low = split(value)
+                    top = dx * 192 + c * 64
+                    upper[top : top + 32, dy * CLUSTERS : (dy + 1) * CLUSTERS] = high
+                    upper[top + 32 : top + 64, dy * CLUSTERS : (dy + 1) * CLUSTERS] = low
         total = mm_nt(upper[...], hot[zs])
         for c in range(3):
-            plane = total[c * 64 : c * 64 + 32] + total[c * 64 + 32 : c * 64 + 64]
+            plane = jnp.zeros((32, G), F32)
+            for dx in range(3):
+                top = dx * 192 + c * 64
+                part = total[top : top + 32] + total[top + 32 : top + 64]
+                plane += pltpu.roll(part, 32 * dx, 1) if dx else part
             for peer in range(WIDTH):
                 sent1[peer, zs, c] = plane[peer * 8 : peer * 8 + 8]
 
@@ -309,15 +319,31 @@
         lax.fori_loop(1, WIDTH, send, 0)
 
     loads[1].wait()
-    build(z_index)
+    loads[2].wait()
 
     def next_slab(i, carry):
-        j = near_first(i)
-        slab_copy(j).wait_recv()
-        build(z_peer(DEPTH - j))
-        return carry
-
-    lax.fori_loop(1, DEPTH, next_slab, 0)
+        @pl.when(i == 1)
+        def _():
+            slab_copy(3).start()
+            slab_copy(4).start()
+
+        @pl.when(i >= 1)
+        def _():
+            slab_copy(i).wait_recv()
+
+        @pl.when(i == 2)
+        def _():
+            slab_copy(5).start()
+            slab_copy(6).start()
+
+        @pl.when(i == 4)
+        def _():
+            slab_copy(7).start()
+
+        build(z_peer(distance(i)))
+        return carry
+
+    lax.fori_loop(0, DEPTH, next_slab, 0)
     got1[x_index] = sent1[x_index]
 
     def copy(stage, c, source, target, device):
@@ -350,7 +376,7 @@
         return lanes_table[k, 0], lanes_table[k, 1]
 
     planes = plane_copy(sent1.at[pl.ds(0, WIDTH - 1)], got1.at[pl.ds(0, WIDTH - 1)], at_x(x_peer(1)))
-    for load in loads[2:5]:
+    for load in loads[3:6]:
         load.wait()
     planes.wait_recv()
 
@@ -362,7 +388,7 @@
 
     lax.fori_loop(0, 3, first_dimension, 0)
 
-    loads[5].wait()
+    loads[6].wait()
     near_sent[...] = jnp.zeros_like(near_sent)
     picked[...] = jnp.zeros_like(picked)
     nobody = jnp.full((3, PANELS), -1, jnp.int32)
@@ -410,7 +436,7 @@
     for near_copy in near_copies:
         near_copy.start()
 
-    loads[6].wait()
+    loads[7].wait()
     below = jnp.zeros((32 - STENCIL, PANELS), F32)
 
     def halve(i, carry):
@@ -473,19 +499,27 @@
     def sample(c, carry):
         whole(2, c, sent4, got4).wait_recv()
 
-        def slab(zs, carry):
-            high, low = split(got4[c, :, zs].reshape(32, G))
-            both = mm(jnp.concatenate([high, low], axis=0), hot[zs])
-            both = both[:32] + both[32:]
-            for d in range(9):
-                part = both[:, d * CLUSTERS : (d + 1) * CLUSTERS]
-                for dz in range(3):
-                    total = jnp.sum(part * phases[zs, dz], axis=0, keepdims=True)
-                    sent5[c, zs, 3 * d + dz : 3 * d + dz + 1] = total
+        def slab(i, carry):
+            zs = z_peer(distance(DEPTH - 1 - i))
+            here = got4[c, :, zs].reshape(32, G)
+            shifted = jnp.concatenate([here] + [pltpu.roll(here, G - 32 * dx, 1) for dx in (1, 2)], axis=0)
+            high, low = split(shifted)
+            both = mm(high, hot[zs]) + mm(low, hot[zs])
+            for dx in range(3):
+                for dy in range(3):
+                    part = both[dx * 32 : dx * 32 + 32, dy * CLUSTERS : (dy + 1) * CLUSTERS]
+                    for dz in range(3):
+                        point = 9 * dx + 3 * dy + dz
+                        sent5[c, zs, point : point + 1] = jnp.sum(part * phases[zs, dz], axis=0, keepdims=True)
+
+            @pl.when(i < DEPTH - 1)
+            def _():
+                copy(3, c, sent5.at[c, zs], got5.at[c, z_index], at_z(zs)).start()
+
             return carry
 
-        lax.fori_loop(0, DEPTH, slab, 0)
-        to_all(3, c, sent5, got5, DEPTH, z_index, z_peer, at_z)
+        lax.fori_loop(0, DEPTH, slab, 0, unroll=2)
+        got5[c, z_index] = sent5[c, z_index]
         return carry
 
     lax.fori_loop(0, 3, sample, 0)
@@ -524,10 +558,13 @@
         at = pl.ds(pl.multiple_of(i * GROUP, GROUP), GROUP)
         for c in range(3):
             far = both[c * 2 * GROUP : c * 2 * GROUP + GROUP] + both[c * 2 * GROUP + GROUP : (c + 1) * 2 * GROUP]
-            out[c, at] = far + near_term[at, c * PANELS : (c + 1) * PANELS]
-        return carry
-
-    lax.fori_loop(0, CLUSTERS // GROUP, project, 0)
+            far += near_term[at, c * PANELS : (c + 1) * PANELS]
+            for k in range(GROUP):
+                place = pl.multiple_of((i * GROUP + k) * PANELS, PANELS)
+                out[c : c + 1, pl.ds(place, PANELS)] = far[k : k + 1]
+        return carry
+
+    lax.fori_loop(0, CLUSTERS // GROUP, project, 0, unroll=8)
 
 
 VMEM = pl.BlockSpec(memory_space=pltpu.VMEM)
@@ -543,24 +580,24 @@
 def per_device(
     density, interp_weight, proj_weight, stencil_corner, near_tiles, pair_target, pair_landing, pair_count
 ):
-    line, rows_table, lanes_table, twiddle = (jnp.asarray(t) for t in make_tables())
+    line, onward, rows_table, lanes_table, twiddle = (jnp.asarray(t) for t in make_tables())
     planes, by_cols = (WIDTH, DEPTH, 3, 8, G), (3, COLS, 32, G)
     by_width, by_depth = (3, WIDTH, DEPTH, 8, G), (3, DEPTH, 32, CLUSTERS)
-    held = (density, interp_weight, proj_weight, line, rows_table, lanes_table, twiddle, near_tiles)
+    held = (density, interp_weight, proj_weight, line, onward, rows_table, lanes_table, twiddle, near_tiles)
     weights = pltpu.VMEM((CLUSTERS // GROUP, G, PANELS), BF16)
-    out = pl.pallas_call(
+    return pl.pallas_call(
         whole_kernel,
-        out_shape=shape((3, CLUSTERS, PANELS)),
-        in_specs=[VMEM] + [SMEM] * 3 + [ANY] * 8,
+        out_shape=shape((3, CLUSTERS * PANELS)),
+        in_specs=[VMEM] + [SMEM] * 3 + [ANY] * 9,
         out_specs=VMEM,
         scratch_shapes=[
             *(pltpu.VMEM(array.shape, array.dtype) for array in held),
             pltpu.VMEM((PACKED, CLUSTERS), F32),
             pltpu.VMEM((SLOTS, 8, PANELS), F32),
             pltpu.VMEM((DEPTH, PACKED, CLUSTERS), F32),
-            pltpu.VMEM((DEPTH, G, 9 * CLUSTERS), BF16),
+            pltpu.VMEM((DEPTH, G, 3 * CLUSTERS), BF16),
             pltpu.VMEM((DEPTH, 3, 32, CLUSTERS), F32),
-            pltpu.VMEM((192, 9 * CLUSTERS), BF16),
+            pltpu.VMEM((576, 3 * CLUSTERS), BF16),
             pltpu.VMEM(planes, F32),
             pltpu.VMEM(planes, F32),
             pltpu.VMEM(by_cols, F32),
@@ -579,7 +616,7 @@
             weights,
             weights,
             pltpu.VMEM((CLUSTERS // GROUP, 3, 2 * GROUP, G), BF16),
-            pltpu.SemaphoreType.DMA((PIECES + 7,)),
+            pltpu.SemaphoreType.DMA((PIECES + 8,)),
             pltpu.SemaphoreType.DMA((DEPTH,)),
             pltpu.SemaphoreType.DMA((DEPTH,)),
             pltpu.SemaphoreType.DMA((2,)),
@@ -591,7 +628,6 @@
             vmem_limit_bytes=LIMIT, collective_id=0, has_side_effects=True
         ),
     )(stencil_corner, pair_target, pair_landing, pair_count, *held)
-    return out.reshape(3, CLUSTERS * PANELS)
 
 
 def solution(mesh):

time: 71.2 us -> 67 us (0.941)
  Pallas kernels: 68.6 us -> 64.5 us
    pallas_call x1, Pallas kernels: 68.6 us -> 64.5 us  [per_device(): pl.pallas_call(whole_kernel, out_shape=shape((3, CLUSTERS * PANELS)), in_...]
where the time goes in v3:
time: 67 us; the launch traced here: 66.8 us
  Pallas kernels  64.5 us (96%)
  local copies, waits for them, and re-layouts  1.7 us (3%)
    pallas_call x1, Pallas kernels, per_device(): pl.pallas_call(whole_kernel, out_shape=shape((3, CLUSTERS * PANELS)), in_...  64.5 us
    unnamed x1, local copies, waits for them, and re-layouts  1.7 us

profile of v3, /device:TPU:1, one launch (start us, length us, event | category | flops | bytes accessed | tf_op | source)
XLA Modules:
  0.0 66.8 jit_solution(3245321675710689335)
XLA Ops:
  0.7 64.5 %shard_map.127 = f32[3,16384]{1,0:T(4,128)} custom-call(s32[3,128]{1,0:T(4,128)} %corner.1, s32[12]{0:T(128)} %target.1, s32[12]{0:T(128)} %landing.1, s32[1]{0:T(128)S(6)} %copy.15.count, f32[3,16384]{1,0:T(4,128)} %density_in.1, f32[27,16384]{1,0:T(8,128)} %interp_in.1, f32[27,16384]{1,0:T(8,128)} %proj_in.1, bf16[8,64,256]{2,1,0:T(8,128)(2,1)} %constant.10.clone.line_in, ...), custom_call_target="tpu_custom_call" | custom-call | tf_op jit(solution)/shard_map/pallas_call | solution.py:588
  65.1 1.7 %copy.16 = f32[3,16384]{1,0:T(4,128)} copy(f32[3,16384]{1,0:T(4,128)} %shard_map.127) | data formatting | bytes 393216

commit v4 on v3

--- a/solution.py
+++ b/solution.py
@@ -18,6 +18,7 @@
 PACKED = 88
 PIECES = 4
 GROUP = 8
+HALF = 128
 CLUSTERS = 128
 PANELS = 128
 SLOTS = 12
@@ -43,32 +44,40 @@
     two_pi = 2 * np.pi
     bins, cells = np.arange(128), np.arange(G)
     theta = two_pi * (bins[:, None] * cells[None, :] % G) / G
-    line = np.stack([np.cos(theta), -np.sin(theta)]).reshape(2, DEPTH, WIDTH, 4, G)
+    line = np.stack([np.cos(theta), -np.sin(theta)]).reshape(2, DEPTH, 4, 4, G)
     line = line.transpose(1, 2, 0, 3, 4).reshape(DEPTH, 32, G)
     line = halves(line).transpose(1, 0, 2, 3).reshape(DEPTH, 64, G)
-    step = 2 * np.pi * np.arange(128).reshape(DEPTH, WIDTH, 1, 4) / G
+    step = 2 * np.pi * np.arange(128).reshape(DEPTH, 4, 1, 4) / G
     onward = np.stack([np.cos(step) + np.zeros((2, 1)), np.sin(step) * np.array([[1.0], [-1.0]])], axis=1)
     onward = np.broadcast_to(onward.reshape(DEPTH, 2, 32, 1), (DEPTH, 2, 32, CLUSTERS)).astype(np.float32)
     eight = np.arange(8)
     wide = np.arange(32)
     turn8 = rotation(two_pi * (eight[:, None] * eight[None, :] % 8) / 8)
     turn32 = rotation(two_pi * (wide[:, None] * wide[None, :] % 32) / 32)
-    second = np.einsum("oipc,hg,lm->pholcgim", turn8, np.eye(4), np.eye(4)).reshape(G, G)
-    by_block = turn32.reshape(2, 2, 32, DEPTH, WIDTH)
-    first = np.einsum("oipzx,lm->polxzim", by_block, np.eye(4)).reshape(G, G)
+    second = np.einsum("oipc,hg,lm->pholcgim", turn8, np.eye(2), np.eye(4)).reshape(HALF, HALF)
+    by_block = turn32.reshape(2, 2, 16, 2, DEPTH, WIDTH)
+    first = []
+    for z in range(DEPTH):
+        order = [(z + d) % DEPTH for d in (0, 7, 1, 6, 2, 5, 3, 4)]
+        mine = by_block[:, :, :, :, order]
+        first_a = np.einsum("oihlabx,km->holkxaibm", mine.reshape(2, 2, 16, 2, 4, 2, WIDTH), np.eye(2))
+        first_b = np.einsum("oihlabx,km->holkxmaib", mine.reshape(2, 2, 16, 2, 2, 4, WIDTH), np.eye(2))
+        both = [t.reshape(HALF, HALF) for t in (first_a, first_b)]
+        first.append(np.stack([halves(t) for t in (*both, both[0].T, both[1].T)]))
+    first = np.stack(first)
     lane32 = [np.kron(np.eye(8), f(two_pi * (wide[:, None] * wide[None, :] % 32) / 32)) for f in (np.cos, np.sin)]
     lane8 = [np.kron(f(two_pi * (eight[:, None] * eight[None, :] % 8) / 8), np.eye(32)) for f in (np.cos, np.sin)]
-    row = np.arange(G)
+    row = np.arange(HALF)
     lane = np.arange(G)
     part_sign = np.where(row // 4 % 2 == 0, 1.0, -1.0)[:, None]
-    twist_y = two_pi * ((row // 32)[:, None] * (lane % 32)[None, :]) / G
-    twist_x = two_pi * ((row // 8)[:, None] * (lane // 32)[None, :]) / G
+    twist_y = two_pi * ((row // 16)[:, None] * (lane % 32)[None, :]) / G
+    twist_x = two_pi * ((row // 8 * 2 + row // 2 % 2)[:, None] * (lane // 32)[None, :]) / G
     twiddle = np.stack(
         [np.cos(twist_y), part_sign * np.sin(twist_y), np.cos(twist_x), part_sign * np.sin(twist_x)]
     ).astype(np.float32)
-    rows_table = np.stack([halves(t) for t in (second, first, first.T, second.T)])
+    second = np.stack([halves(t) for t in (second, second.T)])
     lanes_table = np.stack([halves(np.concatenate(t, axis=1)) for t in (lane32, lane8)])
-    return line, np.ascontiguousarray(onward), rows_table, lanes_table, twiddle
+    return line, np.ascontiguousarray(onward), first, second, lanes_table, twiddle
 
 
 def split(values):
@@ -91,17 +100,36 @@
 
 def on_rows(table_high, table_low, values):
     high, low = split(values)
-    return mm(table_high, high) + (mm(table_low, high) + mm(table_high, low))
+    both = mm(jnp.concatenate([table_high, table_low], axis=0), high)
+    return both[:HALF] + (both[HALF:] + mm(table_high, low))
 
 
 def on_lanes(values, table_high, table_low, sign):
     high, low = split(values)
-    both = mm(high, table_high) + (mm(low, table_high) + mm(high, table_low))
+    both = mm(jnp.concatenate([high, low], axis=0), table_high)
+    both = both[:HALF] + (both[HALF:] + mm(high, table_low))
     return both[:, :G] + sign * swap(both[:, G:])
 
 
+def row_sums(tiles):
+    row = lax.broadcasted_iota(jnp.int32, (8, CLUSTERS), 0)
+    for step in (4, 2, 1):
+        clear = (row & step) == 0
+        merged = []
+        for j in range(step):
+            here = jnp.where(clear, tiles[j], tiles[j + step])
+            there = jnp.where(clear, tiles[j + step], tiles[j])
+            if step == 4:
+                moved = pltpu.roll(there, 4, 0)
+            else:
+                moved = jnp.where(clear, pltpu.roll(there, 8 - step, 0), pltpu.roll(there, step, 0))
+            merged.append(here + moved)
+        tiles = merged
+    return tiles[0]
+
+
 def signs(direction):
-    row = lax.broadcasted_iota(jnp.int32, (G, G), 0)
+    row = lax.broadcasted_iota(jnp.int32, (HALF, G), 0)
     return jnp.where((row & 4) == 0, direction, -direction).astype(F32)
 
 
@@ -121,17 +149,17 @@
     return jnp.where(index < G // 2, index, index - G).astype(F32)
 
 
-def wavevector(row_index, col_index):
-    row = lax.broadcasted_iota(jnp.int32, (G, G), 0)
-    lane = lax.broadcasted_iota(jnp.int32, (G, G), 1)
-    m1 = 4 * col_index + ((row >> 3) & 3) + (lane & -32)
-    m2 = (row >> 5) + 8 * (lane & 31)
-    m3 = 4 * row_index + (row & 3)
-    return m1, m2, m3
-
-
-def screen(row_index, col_index):
-    m1, m2, m3 = wavevector(row_index, col_index)
+def wavevectors(row_index, col_index):
+    z_index, x_index = row_index // WIDTH, lax.rem(row_index, WIDTH)
+    row = lax.broadcasted_iota(jnp.int32, (HALF, G), 0)
+    lane = lax.broadcasted_iota(jnp.int32, (HALF, G), 1)
+    low, above, q = (row >> 1) & 1, lane & -32, 8 * (lane & 31)
+    ours = 4 * col_index + 2 * ((row >> 3) & 1) + low + above, (row >> 4) + q, 16 * z_index + 2 * x_index + (row & 1)
+    theirs = 2 * (row >> 3) + low + above, 2 * x_index + (row & 1) + q, 16 * z_index + 8 + col_index + 0 * row
+    return ours, theirs
+
+
+def screen(m1, m2, m3):
     w1, w2, w3 = wave(m1), wave(m2), m3.astype(F32)
     squared = w1 * w1 + w2 * w2 + w3 * w3
     kept = jnp.where((m1 == G // 2) | (m2 == G // 2), 0.0, FACTOR).astype(F32)
@@ -160,10 +188,13 @@
 
 
 def whole_kernel(
-    corner, target, landing, count, density_in, interp_in, proj_in, line_in, onward_in, rows_in, lanes_in, twiddle_in, tiles_in,
+    corner, target, landing, count,
+    density_in, interp_in, proj_in, line_in, onward_in, first_in, second_in, lanes_in, twiddle_in, tiles_in,
     out,
-    density, interp, proj, line, onward, rows_table, lanes_table, twiddle, blocks,
-    packed, picked, gathered, hot, phases, upper, sent1, got1, sent2, got2, modes, sent3, got3, sent4, got4, sent5, got5,
+    density, interp, proj, line, onward, first, second, lanes_table, twiddle, blocks,
+    packed, picked, gathered, hot, phases, upper, plane,
+    sent1a, got1a, sent1b, got1b, sent2a, got2a, sent2b, got2b, modes_a, modes_b,
+    sent3a, got3a, sent3b, got3b, sent4a, got4a, sent4b, got4b, sent5, got5,
     near_sent, near_got, near_rows, near_term, proj_high, proj_low, values,
     load_sem, slab_send, slab_recv, plane_sem, send_sem, recv_sem, near_sem,
 ):
@@ -182,7 +213,8 @@
                 (density_in, density),
                 (line_in, line),
                 (onward_in, onward),
-                (rows_in, rows_table),
+                (first_in.at[lax.axis_index("row") // WIDTH], first),
+                (second_in, second),
                 (lanes_in, lanes_table),
                 (twiddle_in, twiddle),
                 (tiles_in, blocks),
@@ -271,14 +303,14 @@
     slab_copy(2).start()
     gathered[z_index] = packed[...]
 
-    def plane_copy(source, target, device):
+    def plane_copy(kind, source, target, device):
         return pltpu.make_async_remote_copy(
-            source, target, plane_sem.at[0], plane_sem.at[1], device_id=device, device_id_type=MESH
+            source, target, plane_sem.at[kind, 0], plane_sem.at[kind, 1], device_id=device, device_id_type=MESH
         )
 
     cell = lax.broadcasted_iota(jnp.int32, (G, CLUSTERS), 0).astype(F32)
 
-    def build(zs):
+    def build(zs, place):
         local, depth = gathered[zs, 81:82], gathered[zs, 82:83]
         at = jnp.where(cell == depth, 1.0, 0.0).astype(BF16)
         both = mm(line[z_index], at)
@@ -303,20 +335,50 @@
                     upper[top + 32 : top + 64, dy * CLUSTERS : (dy + 1) * CLUSTERS] = low
         total = mm_nt(upper[...], hot[zs])
         for c in range(3):
-            plane = jnp.zeros((32, G), F32)
+            sum_of = jnp.zeros((32, G), F32)
             for dx in range(3):
                 top = dx * 192 + c * 64
                 part = total[top : top + 32] + total[top + 32 : top + 64]
-                plane += pltpu.roll(part, 32 * dx, 1) if dx else part
+                sum_of += pltpu.roll(part, 32 * dx, 1) if dx else part
+            plane[place, c] = sum_of.reshape(4, 8, G)
+
+    tile_row = lax.broadcasted_iota(jnp.int32, (8, G), 0)
+
+    def shifted(tile, by):
+        return pltpu.roll(tile, by % 8, 0) if by % 8 else tile
+
+    def mix2(tiles, to):
+        return jnp.where((tile_row & 2) == 0, shifted(tiles[0], -2 * to), shifted(tiles[1], 2 - 2 * to))
+
+    def mix4(tiles, to):
+        mixed = shifted(tiles[0], -to)
+        for j in range(1, 4):
+            mixed = jnp.where((tile_row & 3) == j, shifted(tiles[j], j - to), mixed)
+        return mixed
+
+    def send_quad(quad):
+        for c in range(3):
             for peer in range(WIDTH):
-                sent1[peer, zs, c] = plane[peer * 8 : peer * 8 + 8]
-
-        def send(j, carry):
+                for pair in range(2):
+                    tiles = [plane[2 * pair + b, c, peer // 2] for b in range(2)]
+                    sent1a[peer, 2 * quad + pair, c] = mix2(tiles, peer % 2)
+            for peer in range(COLS):
+                tiles = [plane[j, c, 2 + peer // 4] for j in range(4)]
+                sent1b[peer, quad, c] = mix4(tiles, peer % 4)
+
+        def send_a(j, carry):
             peer = x_peer(j)
-            plane_copy(sent1.at[peer, zs], got1.at[x_index, zs], at_x(peer)).start()
+            pair = pl.ds(2 * quad, 2)
+            plane_copy(0, sent1a.at[peer, pair], got1a.at[x_index, pair], at_x(peer)).start()
             return carry
 
-        lax.fori_loop(1, WIDTH, send, 0)
+        def send_b(j, carry):
+            peer = col_peer(j)
+            plane_copy(1, sent1b.at[peer, quad], got1b.at[col_index, quad], at_col(peer)).start()
+            return carry
+
+        lax.fori_loop(1, WIDTH, send_a, 0)
+        lax.fori_loop(1, COLS, send_b, 0)
 
     loads[1].wait()
     loads[2].wait()
@@ -340,11 +402,17 @@
         def _():
             slab_copy(7).start()
 
-        build(z_peer(distance(i)))
-        return carry
-
-    lax.fori_loop(0, DEPTH, next_slab, 0)
-    got1[x_index] = sent1[x_index]
+        build(z_peer(distance(i)), lax.rem(i, 4))
+        return carry
+
+    def four_slabs(quad, carry):
+        lax.fori_loop(4 * quad, 4 * quad + 4, next_slab, 0)
+        send_quad(quad)
+        return carry
+
+    lax.fori_loop(0, 2, four_slabs, 0)
+    got1a[x_index] = sent1a[x_index]
+    got1b[col_index] = sent1b[col_index]
 
     def copy(stage, c, source, target, device):
         return pltpu.make_async_remote_copy(
@@ -369,26 +437,52 @@
         peers = source.shape[1] - 1
         return copy(stage, c, source.at[c, pl.ds(0, peers)], target.at[c, pl.ds(0, peers)], at_row(1))
 
-    def rows_of(k):
-        return rows_table[k, 0], rows_table[k, 1]
+    def first_of(k):
+        return first[k, 0], first[k, 1]
+
+    def second_of(k):
+        return second[k, 0], second[k, 1]
 
     def lanes_of(k):
         return lanes_table[k, 0], lanes_table[k, 1]
 
-    planes = plane_copy(sent1.at[pl.ds(0, WIDTH - 1)], got1.at[pl.ds(0, WIDTH - 1)], at_x(x_peer(1)))
-    for load in loads[3:6]:
+    def first_forward(values, k):
+        return forward(values.reshape(HALF, G), *first_of(k), *lanes_of(1), twiddle[2], twiddle[3])
+
+    def second_forward(values):
+        return forward(values.reshape(HALF, G), *second_of(0), *lanes_of(0), twiddle[0], twiddle[1])
+
+    def first_backward(values, k):
+        return backward(values.reshape(HALF, G), *first_of(2 + k), *lanes_of(1), twiddle[2], twiddle[3])
+
+    def second_backward(values):
+        return backward(values.reshape(HALF, G), *second_of(1), *lanes_of(0), twiddle[0], twiddle[1])
+
+    def to_cols(stage, c, source, target):
+        to_all(stage, c, source, target, COLS, col_index, col_peer, at_col)
+
+    def to_width(stage, c, source, target):
+        to_all(stage, c, source, target, WIDTH, x_index, x_peer, at_x)
+
+    waits = (
+        plane_copy(0, sent1a.at[pl.ds(0, WIDTH - 1)], got1a.at[pl.ds(0, WIDTH - 1)], at_x(x_peer(1))),
+        plane_copy(1, sent1b.at[pl.ds(0, COLS - 1)], got1b.at[pl.ds(0, COLS - 1)], at_col(col_peer(1))),
+    )
+    for load in loads[3:7]:
         load.wait()
-    planes.wait_recv()
-
-    def first_dimension(c, carry):
-        values = forward(got1[:, :, c].reshape(G, G), *rows_of(1), *lanes_of(1), twiddle[2], twiddle[3])
-        sent2[c] = values.reshape(COLS, 32, G)
-        to_all(0, c, sent2, got2, COLS, col_index, col_peer, at_col)
-        return carry
-
-    lax.fori_loop(0, 3, first_dimension, 0)
-
-    loads[6].wait()
+    for wait in waits:
+        wait.wait_recv()
+
+    def step_one(c, carry):
+        sent2a[c] = first_forward(got1a[:, :, c], 0).reshape(COLS, 16, G)
+        to_cols(0, c, sent2a, got2a)
+        sent2b[c] = second_forward(got1b[:, :, c]).reshape(WIDTH, 32, G)
+        to_width(1, c, sent2b, got2b)
+        return carry
+
+    lax.fori_loop(0, 3, step_one, 0, unroll=3)
+
+    loads[7].wait()
     near_sent[...] = jnp.zeros_like(near_sent)
     picked[...] = jnp.zeros_like(picked)
     nobody = jnp.full((3, PANELS), -1, jnp.int32)
@@ -436,7 +530,7 @@
     for near_copy in near_copies:
         near_copy.start()
 
-    loads[7].wait()
+    loads[8].wait()
     below = jnp.zeros((32 - STENCIL, PANELS), F32)
 
     def halve(i, carry):
@@ -450,36 +544,41 @@
 
     lax.fori_loop(0, CLUSTERS // GROUP, halve, 0)
 
-    w1, w2, w3, inverse, weighting = screen(row_index, col_index)
-
-    def second_dimension(c, carry):
-        whole(0, c, sent2, got2).wait_recv()
-        modes[c] = forward(got2[c].reshape(G, G), *rows_of(0), *lanes_of(0), twiddle[0], twiddle[1])
-        return carry
-
-    lax.fori_loop(0, 3, second_dimension, 0)
-
-    inner = (w1 * modes[0] + w2 * modes[1] + w3 * modes[2]) * inverse
-    for c, w in enumerate((w1, w2, w3)):
-        modes[c] = (modes[c] - w * inner) * weighting
-
-    def second_back(c, carry):
-        values = backward(modes[c], *rows_of(3), *lanes_of(0), twiddle[0], twiddle[1])
-        sent3[c] = values.reshape(COLS, 32, G)
-        to_all(1, c, sent3, got3, COLS, col_index, col_peer, at_col)
-        return carry
-
-    lax.fori_loop(0, 3, second_back, 0)
-
-    def first_back(c, carry):
-        whole(1, c, sent3, got3).wait_recv()
-        values = backward(got3[c].reshape(G, G), *rows_of(2), *lanes_of(1), twiddle[2], twiddle[3])
-        sent4[c] = values.reshape(WIDTH, DEPTH, 8, G)
-        to_all(2, c, sent4, got4, WIDTH, x_index, x_peer, at_x)
-        return carry
-
-    lax.fori_loop(0, 3, first_back, 0)
-    sent5[...] = jnp.zeros_like(sent5)
+    screens = [screen(*index) for index in wavevectors(row_index, col_index)]
+
+    def step_two(c, carry):
+        whole(0, c, sent2a, got2a).wait_recv()
+        whole(1, c, sent2b, got2b).wait_recv()
+        modes_a[c] = second_forward(got2a[c])
+        modes_b[c] = first_forward(got2b[c], 1)
+        return carry
+
+    lax.fori_loop(0, 3, step_two, 0)
+
+    for modes, (w1, w2, w3, inverse, weighting) in zip((modes_a, modes_b), screens):
+        inner = (w1 * modes[0] + w2 * modes[1] + w3 * modes[2]) * inverse
+        for c, w in enumerate((w1, w2, w3)):
+            modes[c] = (modes[c] - w * inner) * weighting
+
+    def step_three(c, carry):
+        sent3a[c] = second_backward(modes_a[c]).reshape(COLS, 16, G)
+        to_cols(2, c, sent3a, got3a)
+        sent3b[c] = first_backward(modes_b[c], 1).reshape(WIDTH, 32, G)
+        to_width(3, c, sent3b, got3b)
+        return carry
+
+    lax.fori_loop(0, 3, step_three, 0, unroll=3)
+
+    def step_four(c, carry):
+        whole(2, c, sent3a, got3a).wait_recv()
+        whole(3, c, sent3b, got3b).wait_recv()
+        sent4a[c] = first_backward(got3a[c], 0).reshape(WIDTH, 4, 8, G)
+        to_width(4, c, sent4a, got4a)
+        sent4b[c] = second_backward(got3b[c]).reshape(COLS, 2, 8, G)
+        to_cols(5, c, sent4b, got4b)
+        return carry
+
+    lax.fori_loop(0, 3, step_four, 0)
 
     for near_copy in near_copies:
         near_copy.wait()
@@ -497,24 +596,41 @@
     near_term[...] = mm(lands, high) + mm(lands, low)
 
     def sample(c, carry):
-        whole(2, c, sent4, got4).wait_recv()
+        whole(4, c, sent4a, got4a).wait_recv()
+        whole(5, c, sent4b, got4b).wait_recv()
+
+        def unpack(quad, carry):
+            for j in range(4):
+                pair, b = 2 * quad + j // 2, j % 2
+                for high in range(2):
+                    plane[4 * quad + j, 0, high] = mix2([got4a[c, 2 * high + k, pair] for k in range(2)], b)
+                    plane[4 * quad + j, 0, 2 + high] = mix4([got4b[c, 4 * high + k, quad] for k in range(4)], j)
+            return carry
+
+        lax.fori_loop(0, 2, unpack, 0)
 
         def slab(i, carry):
-            zs = z_peer(distance(DEPTH - 1 - i))
-            here = got4[c, :, zs].reshape(32, G)
-            shifted = jnp.concatenate([here] + [pltpu.roll(here, G - 32 * dx, 1) for dx in (1, 2)], axis=0)
-            high, low = split(shifted)
-            both = mm(high, hot[zs]) + mm(low, hot[zs])
+            step = DEPTH - 1 - i
+            zs = z_peer(distance(step))
+            here = plane[step, 0].reshape(32, G)
+            around = jnp.concatenate([here] + [pltpu.roll(here, G - 32 * dx, 1) for dx in (1, 2)], axis=0)
+            high, low = split(around)
+            both = mm(jnp.concatenate([high, low], axis=0), hot[zs])
+            both = both[:96] + both[96:]
+            parts = []
             for dx in range(3):
                 for dy in range(3):
                     part = both[dx * 32 : dx * 32 + 32, dy * CLUSTERS : (dy + 1) * CLUSTERS]
                     for dz in range(3):
-                        point = 9 * dx + 3 * dy + dz
-                        sent5[c, zs, point : point + 1] = jnp.sum(part * phases[zs, dz], axis=0, keepdims=True)
+                        product = (part * phases[zs, dz]).reshape(4, 8, CLUSTERS)
+                        parts.append((product[0] + product[1]) + (product[2] + product[3]))
+            parts += [jnp.zeros((8, CLUSTERS), F32)] * (32 - STENCIL)
+            for k in range(4):
+                sent5[c, zs, 8 * k : 8 * k + 8] = row_sums(parts[8 * k : 8 * k + 8])
 
             @pl.when(i < DEPTH - 1)
             def _():
-                copy(3, c, sent5.at[c, zs], got5.at[c, z_index], at_z(zs)).start()
+                copy(6, c, sent5.at[c, zs], got5.at[c, z_index], at_z(zs)).start()
 
             return carry
 
@@ -529,13 +645,17 @@
         return carry
 
     lax.fori_loop(1, DEPTH, send_done, 0)
-    planes.wait_send()
+    for wait in waits:
+        wait.wait_send()
 
     def finish(c, carry):
-        whole(0, c, sent2, got2).wait_send()
-        whole(1, c, sent3, got3).wait_send()
-        whole(2, c, sent4, got4).wait_send()
-        whole(3, c, sent5, got5).wait()
+        whole(0, c, sent2a, got2a).wait_send()
+        whole(1, c, sent2b, got2b).wait_send()
+        whole(2, c, sent3a, got3a).wait_send()
+        whole(3, c, sent3b, got3b).wait_send()
+        whole(4, c, sent4a, got4a).wait_send()
+        whole(5, c, sent4b, got4b).wait_send()
+        whole(6, c, sent5, got5).wait()
         total = jnp.sum(got5[c], axis=0)
         turned = jnp.concatenate([total] * 4, axis=0).T
         both = jnp.concatenate([turned, turned], axis=1)
@@ -580,33 +700,32 @@
 def per_device(
     density, interp_weight, proj_weight, stencil_corner, near_tiles, pair_target, pair_landing, pair_count
 ):
-    line, onward, rows_table, lanes_table, twiddle = (jnp.asarray(t) for t in make_tables())
-    planes, by_cols = (WIDTH, DEPTH, 3, 8, G), (3, COLS, 32, G)
-    by_width, by_depth = (3, WIDTH, DEPTH, 8, G), (3, DEPTH, 32, CLUSTERS)
-    held = (density, interp_weight, proj_weight, line, onward, rows_table, lanes_table, twiddle, near_tiles)
+    line, onward, first, second, lanes_table, twiddle = (jnp.asarray(t) for t in make_tables())
+    planes_a, planes_b = pltpu.VMEM((WIDTH, 4, 3, 8, G), F32), pltpu.VMEM((COLS, 2, 3, 8, G), F32)
+    by_cols, by_width = pltpu.VMEM((3, COLS, 16, G), F32), pltpu.VMEM((3, WIDTH, 32, G), F32)
+    modes = pltpu.VMEM((3, HALF, G), F32)
+    last_a, last_b = pltpu.VMEM((3, WIDTH, 4, 8, G), F32), pltpu.VMEM((3, COLS, 2, 8, G), F32)
+    by_depth = (3, DEPTH, 32, CLUSTERS)
+    held = (density, interp_weight, proj_weight, line, onward, first, second, lanes_table, twiddle, near_tiles)
     weights = pltpu.VMEM((CLUSTERS // GROUP, G, PANELS), BF16)
     return pl.pallas_call(
         whole_kernel,
         out_shape=shape((3, CLUSTERS * PANELS)),
-        in_specs=[VMEM] + [SMEM] * 3 + [ANY] * 9,
+        in_specs=[VMEM] + [SMEM] * 3 + [ANY] * 10,
         out_specs=VMEM,
         scratch_shapes=[
-            *(pltpu.VMEM(array.shape, array.dtype) for array in held),
+            *(pltpu.VMEM(array.shape[1:] if array is first else array.shape, array.dtype) for array in held),
             pltpu.VMEM((PACKED, CLUSTERS), F32),
             pltpu.VMEM((SLOTS, 8, PANELS), F32),
             pltpu.VMEM((DEPTH, PACKED, CLUSTERS), F32),
             pltpu.VMEM((DEPTH, G, 3 * CLUSTERS), BF16),
             pltpu.VMEM((DEPTH, 3, 32, CLUSTERS), F32),
             pltpu.VMEM((576, 3 * CLUSTERS), BF16),
-            pltpu.VMEM(planes, F32),
-            pltpu.VMEM(planes, F32),
-            pltpu.VMEM(by_cols, F32),
-            pltpu.VMEM(by_cols, F32),
-            pltpu.VMEM((3, G, G), F32),
-            pltpu.VMEM(by_cols, F32),
-            pltpu.VMEM(by_cols, F32),
-            pltpu.VMEM(by_width, F32),
-            pltpu.VMEM(by_width, F32),
+            pltpu.VMEM((DEPTH, 3, 4, 8, G), F32),
+            *(planes_a, planes_a, planes_b, planes_b),
+            *(by_cols, by_cols, by_width, by_width, modes, modes),
+            *(by_cols, by_cols, by_width, by_width),
+            *(last_a, last_a, last_b, last_b),
             pltpu.VMEM(by_depth, F32),
             pltpu.VMEM(by_depth, F32),
             pltpu.VMEM((SLOTS, 8, PANELS), F32),
@@ -616,12 +735,12 @@
             weights,
             weights,
             pltpu.VMEM((CLUSTERS // GROUP, 3, 2 * GROUP, G), BF16),
-            pltpu.SemaphoreType.DMA((PIECES + 8,)),
+            pltpu.SemaphoreType.DMA((PIECES + 9,)),
             pltpu.SemaphoreType.DMA((DEPTH,)),
             pltpu.SemaphoreType.DMA((DEPTH,)),
-            pltpu.SemaphoreType.DMA((2,)),
-            pltpu.SemaphoreType.DMA((4, 3)),
-            pltpu.SemaphoreType.DMA((4, 3)),
+            pltpu.SemaphoreType.DMA((2, 2)),
+            pltpu.SemaphoreType.DMA((7, 3)),
+            pltpu.SemaphoreType.DMA((7, 3)),
             pltpu.SemaphoreType.DMA((2, 8)),
         ],
         compiler_params=pltpu.CompilerParams(

time: 67 us -> 64.7 us (0.966)
  Pallas kernels: 64.5 us -> 62.1 us
    pallas_call x1, Pallas kernels: 64.5 us -> 62.1 us  [per_device(): pl.pallas_call(whole_kernel, out_shape=shape((3, CLUSTERS * PANELS)), in_...]
where the time goes in v4:
time: 64.7 us; the launch traced here: 64.5 us
  Pallas kernels  62.1 us (96%)
  local copies, waits for them, and re-layouts  1.7 us (3%)
  between operations  0.66 us (1%)
    pallas_call x1, Pallas kernels, per_device(): pl.pallas_call(whole_kernel, out_shape=shape((3, CLUSTERS * PANELS)), in_...  62.1 us
    unnamed x1, local copies, waits for them, and re-layouts  1.7 us

profile of v4, /device:TPU:1, one launch (start us, length us, event | category | flops | bytes accessed | tf_op | source)
XLA Modules:
  0.0 64.5 jit_solution(7205860274944710396)
XLA Ops:
  0.7 62.1 %shard_map.136 = f32[3,16384]{1,0:T(4,128)} custom-call(s32[3,128]{1,0:T(4,128)} %corner.1, s32[12]{0:T(128)} %target.1, s32[12]{0:T(128)} %landing.1, s32[1]{0:T(128)S(6)} %copy.16.count, f32[3,16384]{1,0:T(4,128)} %density_in.1, f32[27,16384]{1,0:T(8,128)} %interp_in.1, f32[27,16384]{1,0:T(8,128)} %proj_in.1, bf16[8,64,256]{2,1,0:T(8,128)(2,1)} %constant.12.clone.line_in, ...), custom_call_target="tpu_custom_call" | custom-call | tf_op jit(solution)/shard_map/pallas_call | solution.py:711
  62.8 1.7 %copy.17 = f32[3,16384]{1,0:T(4,128)} copy(f32[3,16384]{1,0:T(4,128)} %shard_map.136) | data formatting | bytes 393216

commit v5 on v4

--- a/solution.py
+++ b/solution.py
@@ -301,6 +301,8 @@
 
     slab_copy(1).start()
     slab_copy(2).start()
+    slab_copy(3).start()
+    slab_copy(4).start()
     gathered[z_index] = packed[...]
 
     def plane_copy(kind, source, target, device):
@@ -386,21 +388,13 @@
     def next_slab(i, carry):
         @pl.when(i == 1)
         def _():
-            slab_copy(3).start()
-            slab_copy(4).start()
+            slab_copy(5).start()
+            slab_copy(6).start()
+            slab_copy(7).start()
 
         @pl.when(i >= 1)
         def _():
             slab_copy(i).wait_recv()
-
-        @pl.when(i == 2)
-        def _():
-            slab_copy(5).start()
-            slab_copy(6).start()
-
-        @pl.when(i == 4)
-        def _():
-            slab_copy(7).start()
 
         build(z_peer(distance(i)), lax.rem(i, 4))
         return carry
@@ -594,6 +588,9 @@
     lands = lands.astype(BF16)
     high, low = split(near_rows[...])
     near_term[...] = mm(lands, high) + mm(lands, low)
+
+    points = pl.ds(0, STENCIL)
+    others = pl.ds(0, DEPTH - 1)
 
     def sample(c, carry):
         whole(4, c, sent4a, got4a).wait_recv()
@@ -630,7 +627,7 @@
 
             @pl.when(i < DEPTH - 1)
             def _():
-                copy(6, c, sent5.at[c, zs], got5.at[c, z_index], at_z(zs)).start()
+                copy(6, c, sent5.at[c, zs, points], got5.at[c, z_index, points], at_z(zs)).start()
 
             return carry
 
@@ -655,8 +652,9 @@
         whole(3, c, sent3b, got3b).wait_send()
         whole(4, c, sent4a, got4a).wait_send()
         whole(5, c, sent4b, got4b).wait_send()
-        whole(6, c, sent5, got5).wait()
-        total = jnp.sum(got5[c], axis=0)
+        copy(6, c, sent5.at[c, others, points], got5.at[c, others, points], at_row(1)).wait()
+        total = jnp.sum(got5[c, :, :STENCIL], axis=0)
+        total = jnp.concatenate([total, below], axis=0)
         turned = jnp.concatenate([total] * 4, axis=0).T
         both = jnp.concatenate([turned, turned], axis=1)
         both = jnp.where(own, both, jnp.zeros_like(both))

time: 64.7 us -> 62.1 us (0.960)
  Pallas kernels: 62.1 us -> 59.6 us
    pallas_call x1, Pallas kernels: 62.1 us -> 59.6 us  [per_device(): pl.pallas_call(whole_kernel, out_shape=shape((3, CLUSTERS * PANELS)), in_...]
where the time goes in v5:
time: 62.1 us; the launch traced here: 61.9 us
  Pallas kernels  59.6 us (96%)
  local copies, waits for them, and re-layouts  1.7 us (3%)
  between operations  0.66 us (1%)
    pallas_call x1, Pallas kernels, per_device(): pl.pallas_call(whole_kernel, out_shape=shape((3, CLUSTERS * PANELS)), in_...  59.6 us
    unnamed x1, local copies, waits for them, and re-layouts  1.7 us

profile of v5, /device:TPU:1, one launch (start us, length us, event | category | flops | bytes accessed | tf_op | source)
XLA Modules:
  0.0 61.9 jit_solution(15670825745638601634)
XLA Ops:
  0.7 59.6 %shard_map.136 = f32[3,16384]{1,0:T(4,128)} custom-call(s32[3,128]{1,0:T(4,128)} %corner.1, s32[12]{0:T(128)} %target.1, s32[12]{0:T(128)} %landing.1, s32[1]{0:T(128)S(6)} %copy.16.count, f32[3,16384]{1,0:T(4,128)} %density_in.1, f32[27,16384]{1,0:T(8,128)} %interp_in.1, f32[27,16384]{1,0:T(8,128)} %proj_in.1, bf16[8,64,256]{2,1,0:T(8,128)(2,1)} %constant.12.clone.line_in, ...), custom_call_target="tpu_custom_call" | custom-call | tf_op jit(solution)/shard_map/pallas_call | solution.py:709
  60.2 1.7 %copy.17 = f32[3,16384]{1,0:T(4,128)} copy(f32[3,16384]{1,0:T(4,128)} %shard_map.136) | data formatting | bytes 393216

commit v6 on v5

--- a/solution.py
+++ b/solution.py
@@ -16,6 +16,7 @@
 DEPTH = 8
 WIDTH = 4
 PACKED = 88
+USED = 83
 PIECES = 4
 GROUP = 8
 HALF = 128
@@ -291,8 +292,8 @@
 
     def slab_copy(i):
         return pltpu.make_async_remote_copy(
-            packed,
-            gathered.at[z_index],
+            packed.at[pl.ds(0, USED)],
+            gathered.at[z_index, pl.ds(0, USED)],
             slab_send.at[i],
             slab_recv.at[i],
             device_id=at_z(z_peer(DEPTH - distance(i))),
@@ -631,7 +632,7 @@
 
             return carry
 
-        lax.fori_loop(0, DEPTH, slab, 0, unroll=2)
+        lax.fori_loop(0, DEPTH, slab, 0, unroll=4)
         got5[c, z_index] = sent5[c, z_index]
         return carry
 

time: 62.1 us -> 61.6 us (level)
  no operation moved by 1% of the time
where the time goes in v6:
time: 61.6 us; the launch traced here: 61.4 us
  Pallas kernels  59 us (96%)
  local copies, waits for them, and re-layouts  1.7 us (3%)
  between operations  0.66 us (1%)
    pallas_call x1, Pallas kernels, per_device(): pl.pallas_call(whole_kernel, out_shape=shape((3, CLUSTERS * PANELS)), in_...  59 us
    unnamed x1, local copies, waits for them, and re-layouts  1.7 us

profile of v6, /device:TPU:1, one launch (start us, length us, event | category | flops | bytes accessed | tf_op | source)
XLA Modules:
  0.0 61.4 jit_solution(15758346968758748598)
XLA Ops:
  0.7 59.0 %shard_map.136 = f32[3,16384]{1,0:T(4,128)} custom-call(s32[3,128]{1,0:T(4,128)} %corner.1, s32[12]{0:T(128)} %target.1, s32[12]{0:T(128)} %landing.1, s32[1]{0:T(128)S(6)} %copy.16.count, f32[3,16384]{1,0:T(4,128)} %density_in.1, f32[27,16384]{1,0:T(8,128)} %interp_in.1, f32[27,16384]{1,0:T(8,128)} %proj_in.1, bf16[8,64,256]{2,1,0:T(8,128)(2,1)} %constant.12.clone.line_in, ...), custom_call_target="tpu_custom_call" | custom-call | tf_op jit(solution)/shard_map/pallas_call | solution.py:710
  59.7 1.7 %copy.17 = f32[3,16384]{1,0:T(4,128)} copy(f32[3,16384]{1,0:T(4,128)} %shard_map.136) | data formatting | bytes 393216

commit v7 on v6

--- a/solution.py
+++ b/solution.py
@@ -564,17 +564,6 @@
 
     lax.fori_loop(0, 3, step_three, 0, unroll=3)
 
-    def step_four(c, carry):
-        whole(2, c, sent3a, got3a).wait_recv()
-        whole(3, c, sent3b, got3b).wait_recv()
-        sent4a[c] = first_backward(got3a[c], 0).reshape(WIDTH, 4, 8, G)
-        to_width(4, c, sent4a, got4a)
-        sent4b[c] = second_backward(got3b[c]).reshape(COLS, 2, 8, G)
-        to_cols(5, c, sent4b, got4b)
-        return carry
-
-    lax.fori_loop(0, 3, step_four, 0)
-
     for near_copy in near_copies:
         near_copy.wait()
     near_rows[...] = jnp.zeros_like(near_rows)
@@ -589,6 +578,18 @@
     lands = lands.astype(BF16)
     high, low = split(near_rows[...])
     near_term[...] = mm(lands, high) + mm(lands, low)
+
+    def step_four(c, carry):
+        whole(2, c, sent3a, got3a).wait_recv()
+        whole(3, c, sent3b, got3b).wait_recv()
+        sent4a[c] = first_backward(got3a[c], 0).reshape(WIDTH, 4, 8, G)
+        to_width(4, c, sent4a, got4a)
+        sent4b[c] = second_backward(got3b[c]).reshape(COLS, 2, 8, G)
+        to_cols(5, c, sent4b, got4b)
+        return carry
+
+    lax.fori_loop(0, 3, step_four, 0)
+
 
     points = pl.ds(0, STENCIL)
     others = pl.ds(0, DEPTH - 1)

time: 61.6 us -> 61.6 us (level)
  no operation moved by 1% of the time
where the time goes in v7:
time: 61.6 us; the launch traced here: 61.4 us
  Pallas kernels  59 us (96%)
  local copies, waits for them, and re-layouts  1.7 us (3%)
  between operations  0.66 us (1%)
    pallas_call x1, Pallas kernels, per_device(): pl.pallas_call(whole_kernel, out_shape=shape((3, CLUSTERS * PANELS)), in_...  59 us
    unnamed x1, local copies, waits for them, and re-layouts  1.7 us

profile of v7, /device:TPU:1, one launch (start us, length us, event | category | flops | bytes accessed | tf_op | source)
XLA Modules:
  0.0 61.4 jit_solution(246368203879603640)
XLA Ops:
  0.7 59.0 %shard_map.136 = f32[3,16384]{1,0:T(4,128)} custom-call(s32[3,128]{1,0:T(4,128)} %corner.1, s32[12]{0:T(128)} %target.1, s32[12]{0:T(128)} %landing.1, s32[1]{0:T(128)S(6)} %copy.16.count, f32[3,16384]{1,0:T(4,128)} %density_in.1, f32[27,16384]{1,0:T(8,128)} %interp_in.1, f32[27,16384]{1,0:T(8,128)} %proj_in.1, bf16[8,64,256]{2,1,0:T(8,128)(2,1)} %constant.12.clone.line_in, ...), custom_call_target="tpu_custom_call" | custom-call | tf_op jit(solution)/shard_map/pallas_call | solution.py:711
  59.7 1.7 %copy.17 = f32[3,16384]{1,0:T(4,128)} copy(f32[3,16384]{1,0:T(4,128)} %shard_map.136) | data formatting | bytes 393216
